TPU v7x, 512 devices: a whole 4x8x8 slice. The times are simulated.
512 devices in a mesh: src: 16 (over z, core), mod: 32 (over x, y).
Axes of the slice: x: 4, y: 8, z: 8, core: 2. Of those that a mesh axis runs over, the one named last changes fastest.
Arguments:
- right_side: float32 [16, 128, 16, 128], P(None, 'mod'), may hold values from -8 to 8
- depth_weight: float32 [128, 16, 128], P('mod'), may hold values from 0.25 to 2
- panels: bfloat16 [64, 3072, 32, 128], P('src', 'mod'), may hold values from -0.09375 to 0.09375
- data_weight: float32 [64, 3072], P('src', 'mod'), may hold values from 1 to 10
- footprints: int32 [64, 32], replicated, may hold values from 0 to 2047, as said below
- counts: int32 [64], replicated, may hold values from 768 to 3072, as said below
Outputs:
- solution: float32 [16, 128, 16, 128], P(None, 'mod')
- residual: float32 [16, 128, 16, 128], P(None, 'mod')
Inputs may be any that keep to these rules, and one draw needn't show every extreme that they name: `footprints`: each row names 32 distinct tiles; at most 2 of one row's tiles lie among the 64 tiles of one index of mod, and in every row some index of mod holds 2 of them. `counts`: some transmitter has all 3072 rows live.
All inputs are finite; a program needn't handle non-finite values.
Results may differ from a plain program's by a relative error of at most 0.039.
Values may be sent and summed in bfloat16 or wider, within the bound.
No kernel may reach another device: no remote copies, remote signals or barrier semaphores. Data moves between devices by JAX's collectives and lax.ppermute only.
A program may use at most 64 MiB of HBM per device.

v0:
```python
import jax
import jax.numpy as jnp
from jax import lax
from jax.sharding import PartitionSpec as P

CAP = 2
ITERS = 3


def for_sending(shard):

    def short(part):
        return part.astype(jnp.bfloat16) if part.dtype == jnp.float32 else part

    return jax.tree.map(short, shard)


def with_halo(shard, sides, width):
    for axis, dim in sides:
        count, length = (lax.axis_size(axis), shard.shape[dim])
        up = [(i, (i + 1) % count) for i in range(count - 1)]
        down = [(j, i) for i, j in up]
        last = lax.slice_in_dim(shard, length - width, length, axis=dim)
        initial = lax.slice_in_dim(shard, 0, width, axis=dim)
        before = lax.ppermute(last, axis, up)
        after = lax.ppermute(initial, axis, down)
        shard = jnp.concatenate([before, shard, after], axis=dim)
    return shard


def solve_small(system, target):
    factor = jnp.linalg.cholesky(system)
    return jax.scipy.linalg.cho_solve((factor, True), target)


def inner_block(first, second):
    columns = first.shape[0]
    return jnp.dot(
        first.reshape(columns, -1), second.reshape(columns, -1).T, precision=lax.Precision.HIGHEST
    )


def combine_cols(field, mixing):
    return jnp.einsum("ixyz,ij->jxyz", field, mixing, precision=lax.Precision.HIGHEST)


def owners_ranks(tile_ids, blocks_dev):
    owners = tile_ids // blocks_dev
    position = jnp.arange(tile_ids.shape[1])
    before = (owners[:, :, None] == owners[:, None, :]) & (
        position[None, None, :] < position[None, :, None]
    )
    ranking = jnp.sum(before.astype(jnp.int32), axis=2)
    return (owners, tile_ids - owners * blocks_dev, ranking)


def slot_map(tile_ids, blocks_dev, owner_index):
    owners, within, ranking = owners_ranks(tile_ids, blocks_dev)
    chosen = (owners == owner_index)[:, None, :] & (
        ranking[:, None, :] == jnp.arange(CAP)[None, :, None]
    )
    within_slot = jnp.sum(jnp.where(chosen, within[:, None, :], 0), axis=2)
    filled = jnp.any(chosen, axis=2)
    mapping = filled[:, :, None] & (
        within_slot[:, :, None] == jnp.arange(blocks_dev)[None, None, :]
    )
    return mapping.reshape(-1, blocks_dev).astype(jnp.float32)


def regularize(field, depth_weight):
    padded = with_halo(for_sending(field), (("mod", 1),), 1).astype(field.dtype)
    beside = padded[:, 2:] + padded[:, :-2]
    padded_yz = jnp.pad(field, ((0, 0), (0, 0), (1, 1), (1, 1)))
    beside = beside + padded_yz[:, :, 2:, 1:-1] + padded_yz[:, :, :-2, 1:-1]
    beside = beside + padded_yz[:, :, 1:-1, 2:] + padded_yz[:, :, 1:-1, :-2]
    return (6.0 + depth_weight)[None] * field - beside


def shards(right_side, depth_weight, panels, data_weight, footprints, counts):
    columns, extent_x, extent_y, block_len = right_side.shape
    tx_here, rows_here, foot_len, _ = panels.shape
    mod_count = lax.axis_size("mod")
    blocks_dev = extent_x * extent_y
    mod_index = lax.axis_index("mod")
    src_index = lax.axis_index("src")
    tx_group = lax.dynamic_slice_in_dim(footprints, src_index * tx_here, tx_here, 0)
    group_counts = lax.dynamic_slice_in_dim(counts, src_index * tx_here, tx_here, 0)
    owners, within, ranking = owners_ranks(tx_group, blocks_dev)
    send_map = slot_map(tx_group, blocks_dev, mod_index)
    send_low = send_map.astype(jnp.bfloat16)
    fetch_index = (owners * (tx_here * CAP) + jnp.arange(tx_here)[:, None] * CAP + ranking).reshape(
        -1
    )
    back_map = (
        (owners[None, :, None, :] == jnp.arange(mod_count)[:, None, None, None])
        & (ranking[None, :, None, :] == jnp.arange(CAP)[None, None, :, None])
    ).astype(jnp.bfloat16)
    row_ids = mod_index * rows_here + jnp.arange(rows_here)
    live_rows = (row_ids[None, :] < group_counts[:, None]).astype(jnp.float32)
    row_weight = data_weight * live_rows
    solution = jnp.zeros_like(right_side)
    residual = right_side
    direction = right_side
    norm_now = lax.psum(inner_block(residual, residual), "mod")
    for iteration in range(ITERS):
        lowered = direction.astype(jnp.bfloat16).reshape(columns, blocks_dev, block_len)
        packed = jnp.einsum(
            "sl,klb->ksb", send_low, lowered, preferred_element_type=jnp.float32
        ).astype(jnp.bfloat16)
        arrived = lax.all_gather(packed, "mod", axis=1, tiled=True)
        picked = jnp.take(arrived, fetch_index, axis=1).reshape(
            columns, tx_here, foot_len, block_len
        )
        response = jnp.einsum("trfb,ktfb->trk", panels, picked, preferred_element_type=jnp.float32)
        weighted = (row_weight[:, :, None] * response).astype(jnp.bfloat16)
        partial_value = jnp.einsum(
            "trfb,trk->ktfb", panels, weighted, preferred_element_type=jnp.float32
        ).astype(jnp.bfloat16)
        slotted = jnp.einsum(
            "otcj,ktjb->kotcb", back_map, partial_value, preferred_element_type=jnp.float32
        )
        slotted = slotted.reshape(columns, mod_count * tx_here * CAP, block_len)
        summed = lax.psum_scatter(
            slotted.astype(jnp.bfloat16), "mod", scatter_dimension=1, tiled=True
        ).astype(jnp.float32)
        own_terms = jnp.einsum("ksb,sl->klb", summed, send_map, precision=lax.Precision.HIGHEST)
        cell_terms = lax.psum(own_terms.astype(jnp.bfloat16), "src").astype(jnp.float32)
        image = cell_terms.reshape(columns, extent_x, extent_y, block_len) + regularize(
            direction, depth_weight
        )
        curvature = lax.psum(inner_block(direction, image), "mod")
        alpha = solve_small(curvature, norm_now)
        solution = solution + combine_cols(direction, alpha)
        updated = residual - combine_cols(image, alpha)
        if iteration + 1 < ITERS:
            norm_next = lax.psum(inner_block(updated, updated), "mod")
            beta_block = solve_small(norm_now, norm_next)
            direction = updated + combine_cols(direction, beta_block)
            norm_now = norm_next
        residual = updated
    return (solution, residual)


def solution(mesh):
    placed = (
        P(None, "mod", None, None),
        P("mod", None, None),
        P("src", "mod", None, None),
        P("src", "mod"),
        P(),
        P(),
    )
    return jax.shard_map(
        shards,
        mesh=mesh,
        in_specs=placed,
        out_specs=(P(None, "mod", None, None), P(None, "mod", None, None)),
        check_vma=False,
    )
```

profile of v0, /device:TPU:1, one launch (start us, length us, event | category | flops | bytes accessed | tf_op | source)
XLA Modules:
  0.0 1766.1 jit_solution(9085490576619150589)
XLA Ops:
  9.0 1.4 copy.264
  13.0 76.3 %all-gather.4.cloned.1.call-done = bf16[16,256,128]{2,1,0:T(8,128)(2,1)} async-done(((bf16[16,8,128]{2,1,0:T(8,128)(2,1)}), bf16[16,256,128]{2,1,0:T(8,128)(2,1)}) %all-gather.4.cloned.1.call-update) | async-done | bytes 1048592 | tf_op jit(solution)/shard_map/all_gather | solution.py:110
  89.3 2.9 copy.98
  92.3 2.7 gather_fusion
  95.0 2.0 broadcast_select_fusion.2
  97.0 4.1 fusion.12
  101.1 1.5 fusion
  102.6 1.7 copy.102
  105.0 2.8 collective-permute-start
  107.8 1.3 collective-permute-start.1
  109.1 2.1 copy.96
  111.2 2.4 convolution_bitcast_fusion.9
  114.4 207.4 %reduce-scatter.4.cloned.1.call-done = bf16[16,8,128]{2,0,1:T(8,128)(2,1)} async-done(((bf16[16,256,128]{2,0,1:T(8,128)(2,1)}), bf16[16,8,128]{2,0,1:T(8,128)(2,1)}) %reduce-scatter.4.cloned.1.call-update) | async-done | bytes 32784 | tf_op jit(solution)/shard_map/reduce_scatter | solution.py:123
  324.0 1.8 maximum_convert_fusion
  325.7 117.7 %all-reduce.8.cloned.1.call-done = bf16[16,4,16,128]{3,0,2,1:T(8,128)(2,1)} async-done(((bf16[16,4,16,128]{3,0,2,1:T(8,128)(2,1)}), bf16[16,4,16,128]{3,0,2,1:T(8,128)(2,1)}) %all-reduce.8.cloned.1.call-update) | async-done | bytes 262160 | tf_op jit(solution)/shard_map/psum | solution.py:127
  443.5 2.6 fusion.73
  446.9 2.0 convolution_bitcast_fusion.10
  448.9 115.2 %all-reduce.3 = (f32[16,16]{0,1:T(8,128)S(1)}, f32[16,16]{0,1:T(8,128)S(1)}) all-reduce(f32[16,16]{0,1:T(8,128)S(1)} %convolution_bitcast_fusion.9, f32[16,16]{0,1:T(8,128)S(1)} %convolution_bitcast_fusion.10), channel_id=1, replica_groups=mesh['src'=16,'mod'=32] {'mod'}, use_global_device_ids=true, to_apply=%region_8.11 | all-reduce | flops 512 | bytes 4096 | tf_op jit(solution)/shard_map/psum | solution.py:104
  564.2 1.5 cholesky.89
  567.0 1.2 custom-call.11
  568.7 2.0 convolution_subtract_fusion.2
  572.3 57.2 %psum.66 = f32[16,16]{0,1:T(8,128)S(1)} all-reduce(f32[16,16]{0,1:T(8,128)S(1)} %convolution_bitcast_fusion.7), channel_id=1, replica_groups=mesh['src'=16,'mod'=32] {'mod'}, use_global_device_ids=true, to_apply=%region_9.13 | all-reduce | flops 256 | bytes 2048 | tf_op jit(solution)/shard_map/psum | solution.py:136
  629.5 1.4 cholesky.100
  633.9 2.8 fusion.167
  637.7 107.1 %all-gather.6.cloned.1.call-done = bf16[16,256,128]{2,1,0:T(8,128)(2,1)} async-done(((bf16[16,8,128]{2,1,0:T(8,128)(2,1)}), bf16[16,256,128]{2,1,0:T(8,128)(2,1)}) %all-gather.6.cloned.1.call-update) | async-done | bytes 1048592 | tf_op jit(solution)/shard_map/all_gather | solution.py:110
  744.8 2.9 copy.121
  747.7 2.7 gather_fusion.1
  750.4 2.0 broadcast_select_fusion.1
  752.4 4.1 fusion.15
  756.6 1.5 fusion.1
  758.0 1.7 copy.125
  759.9 1.5 cholesky.122
  764.6 2.8 collective-permute-start.2
  767.4 1.3 collective-permute-start.3
  768.7 208.8 %reduce-scatter.6.cloned.1.call-done = bf16[16,8,128]{2,0,1:T(8,128)(2,1)} async-done(((bf16[16,256,128]{2,0,1:T(8,128)(2,1)}), bf16[16,8,128]{2,0,1:T(8,128)(2,1)}) %reduce-scatter.6.cloned.1.call-update) | async-done | bytes 32784 | tf_op jit(solution)/shard_map/reduce_scatter | solution.py:123
  979.6 1.8 maximum_convert_fusion.1
  981.4 117.2 %all-reduce.10.cloned.1.call-done = bf16[16,4,16,128]{3,0,2,1:T(8,128)(2,1)} async-done(((bf16[16,4,16,128]{3,0,2,1:T(8,128)(2,1)}), bf16[16,4,16,128]{3,0,2,1:T(8,128)(2,1)}) %all-reduce.10.cloned.1.call-update) | async-done | bytes 262160 | tf_op jit(solution)/shard_map/psum | solution.py:127
  1098.6 2.7 fusion.79
  1102.1 1.8 convolution_bitcast_fusion.5
  1103.9 61.7 %psum.68 = f32[16,16]{0,1:T(8,128)S(1)} all-reduce(f32[16,16]{0,1:T(8,128)S(1)} %convolution_bitcast_fusion.5), channel_id=1, replica_groups=mesh['src'=16,'mod'=32] {'mod'}, use_global_device_ids=true, to_apply=%region_12.16 | all-reduce | flops 256 | bytes 2048 | tf_op jit(solution)/shard_map/psum | solution.py:131
  1165.7 1.5 cholesky.111
  1170.3 1.8 convolution_subtract_fusion.1
  1173.7 56.7 %psum.69 = f32[16,16]{1,0:T(8,128)S(1)} all-reduce(f32[16,16]{1,0:T(8,128)S(1)} %convolution_bitcast_fusion.3), channel_id=1, replica_groups=mesh['src'=16,'mod'=32] {'mod'}, use_global_device_ids=true, to_apply=%region_13.17 | all-reduce | flops 256 | bytes 2048 | tf_op jit(solution)/shard_map/psum | solution.py:136
  1230.8 2.6 fusion.168
  1234.5 93.7 %all-gather.8.cloned.1.call-done = bf16[16,256,128]{2,1,0:T(8,128)(2,1)} async-done(((bf16[16,8,128]{2,1,0:T(8,128)(2,1)}), bf16[16,256,128]{2,1,0:T(8,128)(2,1)}) %all-gather.8.cloned.1.call-update) | async-done | bytes 1048592 | tf_op jit(solution)/shard_map/all_gather | solution.py:110
  1328.2 2.9 copy.135
  1331.1 2.8 gather_fusion.2
  1333.9 2.1 broadcast_select_fusion
  1336.0 4.1 fusion.18
  1340.1 1.5 fusion.2
  1341.6 1.7 copy.139
  1343.3 1.9 fusion.159
  1345.8 2.8 collective-permute-start.4
  1348.7 1.3 collective-permute-start.5
  1350.0 2.4 convolution_add_fusion.2
  1352.4 208.7 %reduce-scatter.8.cloned.1.call-done = bf16[16,8,128]{2,0,1:T(8,128)(2,1)} async-done(((bf16[16,256,128]{2,0,1:T(8,128)(2,1)}), bf16[16,8,128]{2,0,1:T(8,128)(2,1)}) %reduce-scatter.8.cloned.1.call-update) | async-done | bytes 32784 | tf_op jit(solution)/shard_map/reduce_scatter | solution.py:123
  1563.2 1.8 maximum_convert_fusion.2
  1565.0 117.7 %all-reduce.12.cloned.1.call-done = bf16[16,4,16,128]{3,0,2,1:T(8,128)(2,1)} async-done(((bf16[16,4,16,128]{3,0,2,1:T(8,128)(2,1)}), bf16[16,4,16,128]{3,0,2,1:T(8,128)(2,1)}) %all-reduce.12.cloned.1.call-update) | async-done | bytes 262160 | tf_op jit(solution)/shard_map/psum | solution.py:127
  1682.7 2.6 fusion.85
  1686.0 1.8 convolution_bitcast_fusion.1
  1687.9 61.7 %psum.71 = f32[16,16]{0,1:T(8,128)S(1)} all-reduce(f32[16,16]{0,1:T(8,128)S(1)} %convolution_bitcast_fusion.1), channel_id=1, replica_groups=mesh['src'=16,'mod'=32] {'mod'}, use_global_device_ids=true, to_apply=%region_16.20 | all-reduce | flops 256 | bytes 2048 | tf_op jit(solution)/shard_map/psum | solution.py:131
  1749.7 1.5 cholesky.133
  1754.1 1.8 convolution_subtract_fusion
  1756.8 1.8 convolution_add_fusion
  (133 shorter events, 37.0 us)
Async XLA Ops:
  7.2 89.8 %copy-start = (bf16[4,96,32,128]{3,2,1,0:T(8,128)(2,1)S(1)}, bf16[4,96,32,128]{3,2,1,0:T(8,128)(2,1)}, u32[]{:S(2)}) copy-start(bf16[4,96,32,128]{3,2,1,0:T(8,128)(2,1)} %param.13) | copy-start | bytes 9437188
  7.2 82.1 %all-gather.4.cloned.1.call-start = ((), (), s32[]{:S(2)}) async-start(), calls=%async_computation.3 | async-start | bytes 1081344 | tf_op jit(solution)/shard_map/all_gather | solution.py:110
  8.9 627.8 %copy-start.6 = (s32[8]{0:T(128)}, s32[8]{0:T(128)S(1)}, u32[]{:S(2)}) copy-start(s32[8]{0:T(128)S(1)} %eq.93) | copy-start | bytes 100
  9.0 312.9 %copy-start.10 = (pred[8]{0:T(512)(128)(4,1)}, pred[8]{0:T(512)(128)(4,1)S(1)}, u32[]{:S(2)}) copy-start(pred[8]{0:T(512)(128)(4,1)S(1)} %and.61) | copy-start | bytes 28
  11.2 310.7 %reduce-scatter.4.cloned.1.call-start = ((), (), s32[]{:S(2)}) async-start(), calls=%async_computation.4 | async-start | bytes 1081344 | tf_op jit(solution)/shard_map/reduce_scatter | solution.py:123
  12.2 735.5 %copy-start.9 = (s32[1024]{0:T(1024)}, s32[1024]{0:T(1024)S(1)}, u32[]{:S(2)}) copy-start(s32[1024]{0:T(1024)S(1)} %pad_clamp_fusion) | copy-start | bytes 12292
  12.2 88.9 %copy-start.14 = (pred[128]{0:T(512)(128)(4,1)}, pred[128]{0:T(512)(128)(4,1)S(1)}, u32[]{:S(2)}) copy-start(pred[128]{0:T(512)(128)(4,1)S(1)} %compare_and_fusion) | copy-start | bytes 388
  104.3 339.2 %all-reduce.8.cloned.1.call-start = ((), (), s32[]{:S(2)}) async-start(), calls=%async_computation.5 | async-start | bytes 524288 | tf_op jit(solution)/shard_map/psum | solution.py:127
  105.0 219.0 %collective-permute-start = (bf16[16,1,16,128]{3,0,2,1:T(8,128)(2,1)}, bf16[16,1,16,128]{3,0,2,1:T(8,128)(2,1)S(1)}, u32[]{:S(2)}, u32[]{:S(2)}) collective-permute-start(bf16[16,1,16,128]{3,0,2,1:T(8,128)(2,1)} %get-tuple-element.21), channel_id=1, source_target_pairs={{0,1},{1,2},{2,3},{3,4},{4,5},{5,6},{6,7},{7,8},{8,9},{9,10},{10,1... | collective-permute-start | bytes 196616 | tf_op jit(solution)/shard_map/ppermute | solution.py:25
  107.8 216.2 %collective-permute-start.1 = (bf16[16,1,16,128]{3,0,2,1:T(8,128)(2,1)}, bf16[16,1,16,128]{3,0,2,1:T(8,128)(2,1)}, u32[]{:S(2)}, u32[]{:S(2)}) collective-permute-start(bf16[16,1,16,128]{3,0,2,1:T(8,128)(2,1)} %get-tuple-element.22), channel_id=1, source_target_pairs={{1,0},{2,1},{3,2},{4,3},{5,4},{6,5},{7,6},{8,7},{9,8},{10,9},{11,1... | collective-permute-start | bytes 196616 | tf_op jit(solution)/shard_map/ppermute | solution.py:26
  323.9 420.9 %all-gather.6.cloned.1.call-start = ((), (), s32[]{:S(2)}) async-start(), calls=%async_computation.6 | async-start | bytes 1081344 | tf_op jit(solution)/shard_map/all_gather | solution.py:110
  446.1 0.8 copy-start.3
  446.9 189.9 %copy-start.11 = (pred[8]{0:T(512)(128)(4,1)S(1)}, pred[8]{0:T(512)(128)(4,1)}, u32[]{:S(2)}) copy-start(pred[8]{0:T(512)(128)(4,1)} %copy-done.10) | copy-start | bytes 28
  570.7 0.8 copy-start.1
  571.5 178.9 %copy-start.15 = (pred[128]{0:T(512)(128)(4,1)S(1)}, pred[128]{0:T(512)(128)(4,1)}, u32[]{:S(2)}) copy-start(pred[128]{0:T(512)(128)(4,1)} %copy-done.14) | copy-start | bytes 388
  637.6 339.9 %reduce-scatter.6.cloned.1.call-start = ((), (), s32[]{:S(2)}) async-start(), calls=%async_computation.7 | async-start | bytes 1081344 | tf_op jit(solution)/shard_map/reduce_scatter | solution.py:123
  759.7 338.9 %all-reduce.10.cloned.1.call-start = ((), (), s32[]{:S(2)}) async-start(), calls=%async_computation.8 | async-start | bytes 524288 | tf_op jit(solution)/shard_map/psum | solution.py:127
  764.6 215.1 %collective-permute-start.2 = (bf16[16,1,16,128]{3,0,2,1:T(8,128)(2,1)}, bf16[16,1,16,128]{3,0,2,1:T(8,128)(2,1)S(1)}, u32[]{:S(2)}, u32[]{:S(2)}) collective-permute-start(bf16[16,1,16,128]{3,0,2,1:T(8,128)(2,1)} %get-tuple-element.19), channel_id=1, source_target_pairs={{0,1},{1,2},{2,3},{3,4},{4,5},{5,6},{6,7},{7,8},{8,9},{9,10},{10,1... | collective-permute-start | bytes 196616 | tf_op jit(solution)/shard_map/ppermute | solution.py:25
  767.4 212.2 %collective-permute-start.3 = (bf16[16,1,16,128]{3,0,2,1:T(8,128)(2,1)}, bf16[16,1,16,128]{3,0,2,1:T(8,128)(2,1)}, u32[]{:S(2)}, u32[]{:S(2)}) collective-permute-start(bf16[16,1,16,128]{3,0,2,1:T(8,128)(2,1)} %get-tuple-element.20), channel_id=1, source_target_pairs={{1,0},{2,1},{3,2},{4,3},{5,4},{6,5},{7,6},{8,7},{9,8},{10,9},{11,1... | collective-permute-start | bytes 196616 | tf_op jit(solution)/shard_map/ppermute | solution.py:26
  979.6 348.6 %all-gather.8.cloned.1.call-start = ((), (), s32[]{:S(2)}) async-start(), calls=%async_computation.9 | async-start | bytes 1081344 | tf_op jit(solution)/shard_map/all_gather | solution.py:110
  1101.3 0.8 copy-start.5
  1102.1 131.3 %copy-start.7 = (s32[8]{0:T(128)S(1)}, s32[8]{0:T(128)}, u32[]{:S(2)}) copy-start(s32[8]{0:T(128)} %copy-done.6) | copy-start | bytes 100
  1102.1 131.3 %copy-start.12 = (pred[8]{0:T(512)(128)(4,1)S(1)}, pred[8]{0:T(512)(128)(4,1)}, u32[]{:S(2)}) copy-start(pred[8]{0:T(512)(128)(4,1)} %copy-done.10) | copy-start | bytes 28
  1172.1 0.8 copy-start.2
  1172.9 161.1 %copy-start.16 = (pred[128]{0:T(512)(128)(4,1)S(1)}, pred[128]{0:T(512)(128)(4,1)}, u32[]{:S(2)}) copy-start(pred[128]{0:T(512)(128)(4,1)} %copy-done.14) | copy-start | bytes 388
  1234.2 326.9 %reduce-scatter.8.cloned.1.call-start = ((), (), s32[]{:S(2)}) async-start(), calls=%async_computation.10 | async-start | bytes 1081344 | tf_op jit(solution)/shard_map/reduce_scatter | solution.py:123
  1341.6 219.6 %copy-start.8 = (s32[8]{0:T(128)S(1)}, s32[8]{0:T(128)}, u32[]{:S(2)}) copy-start(s32[8]{0:T(128)} %copy-done.6) | copy-start | bytes 100
  1341.6 219.6 %copy-start.13 = (pred[8]{0:T(512)(128)(4,1)S(1)}, pred[8]{0:T(512)(128)(4,1)}, u32[]{:S(2)}) copy-start(pred[8]{0:T(512)(128)(4,1)} %copy-done.10) | copy-start | bytes 28
  1343.3 339.4 %all-reduce.12.cloned.1.call-start = ((), (), s32[]{:S(2)}) async-start(), calls=%async_computation.11 | async-start | bytes 524288 | tf_op jit(solution)/shard_map/psum | solution.py:127
  1345.8 217.3 %collective-permute-start.4 = (bf16[16,1,16,128]{3,0,2,1:T(8,128)(2,1)}, bf16[16,1,16,128]{3,0,2,1:T(8,128)(2,1)S(1)}, u32[]{:S(2)}, u32[]{:S(2)}) collective-permute-start(bf16[16,1,16,128]{3,0,2,1:T(8,128)(2,1)} %get-tuple-element.17), channel_id=1, source_target_pairs={{0,1},{1,2},{2,3},{3,4},{4,5},{5,6},{6,7},{7,8},{8,9},{9,10},{10,1... | collective-permute-start | bytes 196616 | tf_op jit(solution)/shard_map/ppermute | solution.py:25
  1348.7 214.5 %collective-permute-start.5 = (bf16[16,1,16,128]{3,0,2,1:T(8,128)(2,1)}, bf16[16,1,16,128]{3,0,2,1:T(8,128)(2,1)}, u32[]{:S(2)}, u32[]{:S(2)}) collective-permute-start(bf16[16,1,16,128]{3,0,2,1:T(8,128)(2,1)} %get-tuple-element.18), channel_id=1, source_target_pairs={{1,0},{2,1},{3,2},{4,3},{5,4},{6,5},{7,6},{8,7},{9,8},{10,9},{11,1... | collective-permute-start | bytes 196616 | tf_op jit(solution)/shard_map/ppermute | solution.py:26
  1685.2 0.8 copy-start.4
Sparse Core Ops, SparseCore 0:
  11.6 77.6 all-gather.3
  104.4 217.4 reduce-scatter.3
  324.8 118.6 all-reduce.7
  637.7 106.9 all-gather.5
  759.8 217.6 reduce-scatter.5
  979.8 118.7 all-reduce.9
  1234.3 93.7 all-gather.7
  1343.4 217.6 reduce-scatter.7
  1564.0 118.5 all-reduce.11
where the time goes:
time: 1780 us; the launch traced here: 1770 us
  waiting for transfers between devices  1250 us (70%)
  blocking collectives  353 us (20%)
  matrix products  51.2 us (3%)
  other arithmetic  41.7 us (2%)
  local copies, waits for them, and re-layouts  38.4 us (2%)
    reduce_scatter x3, waiting for transfers between devices, shards(): lax.psum_scatter(slotted.astype(jnp.bfloat16), 'mod', scatter_dimension=1...  625 us
    psum x3, waiting for transfers between devices, shards(): lax.psum(own_terms.astype(jnp.bfloat16), 'src').astype(jnp.float32)  353 us
    all_gather x3, waiting for transfers between devices, shards(): arrived = lax.all_gather(packed, 'mod', axis=1, tiled=True)  277 us
    psum x2, blocking collectives, shards(): curvature = lax.psum(inner_block(direction, image), 'mod')  123 us
    psum x1, blocking collectives, shards(): norm_now = lax.psum(inner_block(residual, residual), 'mod')  115 us
    psum x2, blocking collectives, shards(): norm_next = lax.psum(inner_block(updated, updated), 'mod')  114 us
  transfers between devices with their start and end apart: 15, of which 9 were waited for; matrix products, arithmetic and copies ran while one was open for 2% of the time, Pallas kernels for 0%

commit v1 on v0

v1 whole, which is shorter than its diff:
```python
import functools

import jax
import jax.numpy as jnp
from jax import lax
from jax.experimental import pallas as pl
from jax.experimental.pallas import tpu as pltpu
from jax.sharding import PartitionSpec as P

CAP = 2
ITERS = 3
F32 = jnp.float32
BF16 = jnp.bfloat16
VMEM = pl.BlockSpec(memory_space=pltpu.VMEM)
SMEM = pl.BlockSpec(memory_space=pltpu.SMEM)


def call(kernel, outs, args, specs, scratch=(), limit=32 << 20):
    return pl.pallas_call(
        kernel,
        out_shape=[jax.ShapeDtypeStruct(shape, dtype) for shape, dtype in outs],
        in_specs=list(specs),
        out_specs=[VMEM] * len(outs),
        scratch_shapes=list(scratch),
        compiler_params=pltpu.CompilerParams(vmem_limit_bytes=limit),
    )(*args)


def solve_small(system, target):
    size = system.shape[0]
    work = jnp.concatenate([system, target], axis=1)
    rows = lax.broadcasted_iota(jnp.int32, work.shape, 0)
    for j in range(size):
        pivot = work[j : j + 1, :] / work[j : j + 1, j : j + 1]
        work = jnp.where(rows == j, pivot, work - work[:, j : j + 1] * pivot)
    return work[:, size:]


def split_three(gram):
    size = gram.shape[0]
    high = gram.astype(BF16).astype(F32)
    rest = gram - high
    middle = rest.astype(BF16).astype(F32)
    low = rest - middle
    fill = jnp.zeros((size, 128 - 3 * size), F32)
    return jnp.concatenate([high, middle, low, fill], axis=1).astype(BF16)


def join_three(total):
    size = total.shape[0]
    return total[:, :size] + total[:, size : 2 * size] + total[:, 2 * size : 3 * size]


def spread_mixing(mixing):
    size = mixing.shape[0]
    turned = mixing.T
    return [jnp.broadcast_to(turned[:, i : i + 1], (size, 128)) for i in range(size)]


def mix_tile(tile, spread):
    total = None
    for i, factor in enumerate(spread):
        term = factor * tile[i : i + 1, :]
        total = term if total is None else total + term
    return total


def small_dot(first, second, dims):
    return lax.dot_general(
        first, second, (dims, ((), ())), precision=lax.Precision.HIGHEST, preferred_element_type=F32
    )


def halves(value):
    high = value.astype(BF16)
    return high, (value - high.astype(F32)).astype(BF16)


def nt(first, second):
    return lax.dot_general(first, second, (((1,), (1,)), ((), ())), preferred_element_type=F32)


def gram_halves(first, second):
    (fh, fl), (sh, sl) = first, second
    return nt(fh, sh) + (nt(fh, sl) + nt(fl, sh))


def wide(ref, start, count):
    return jnp.concatenate([ref[start + k] for k in range(count)], axis=1)


def gram(first, second):
    tiles, step, total = first.shape[0], 8, None
    for start in range(0, tiles, step):
        one = halves(wide(first, start, step))
        two = one if second is first else halves(wide(second, start, step))
        part = gram_halves(one, two)
        total = part if total is None else total + part
    return total


def pack(residual, own_tile, sent, first_plane, last_plane, copies, slots, plane):
    tiles = residual.shape[0]
    blocks = [residual[own_tile[s]].astype(BF16) for s in range(slots)]
    blocks.append(split_three(gram(residual, residual)))
    for m in range(copies):
        for s in range(slots + 1):
            sent[m * (slots + 1) + s] = blocks[s]
    for y in range(plane):
        first_plane[y] = residual[y].astype(BF16)
        last_plane[y] = residual[tiles - plane + y].astype(BF16)


def begin_kernel(copies, slots, plane, own_tile, residual, sent, first_plane, last_plane):
    pack(residual, own_tile, sent, first_plane, last_plane, copies, slots, plane)


def advance(src_count, slots, slot_tile, groups, residual, smooth, norm, image, fresh):
    tiles = residual.shape[0]
    per = slots + 1
    image[pl.ds(0, tiles)] = smooth[...]

    def add_group(i, curvature):
        for s in range(slots):
            tile = slot_tile[i * slots + s]
            image[tile] = image[tile] + groups[i * per + s].astype(F32)
        return curvature + groups[i * per + slots].astype(F32)

    start = jnp.zeros(groups.shape[1:], F32)
    curvature = join_three(lax.fori_loop(0, src_count, add_group, start))
    alpha = solve_small(curvature, norm[...])
    spread = spread_mixing(alpha)
    for l in range(tiles):
        fresh[l] = residual[l] - mix_tile(image[l], spread)
    return alpha, spread


def step_kernel(
    src_count, copies, slots, plane, slot_tile, own_tile, groups, residual, smooth, norm,
    fresh, alpha_out, sent, first_plane, last_plane, image,
):
    alpha, _ = advance(src_count, slots, slot_tile, groups, residual, smooth, norm, image, fresh)
    alpha_out[...] = alpha
    pack(fresh, own_tile, sent, first_plane, last_plane, copies, slots, plane)


def last_kernel(
    src_count, slots, slot_tile, groups, residual, smooth, norm, direction, solution,
    fresh, solution_out, image,
):
    _, spread = advance(src_count, slots, slot_tile, groups, residual, smooth, norm, image, fresh)
    for l in range(residual.shape[0]):
        solution_out[l] = solution[l] + mix_tile(direction[l], spread)


def smooth_field(field, before, after, diagonal, out, plane):
    tiles = field.shape[0]
    lanes = lax.broadcasted_iota(jnp.int32, field.shape[1:], 1)
    last = field.shape[2] - 1
    for l in range(tiles):
        tile = field[l]
        y = l % plane
        beside = jnp.where(lanes == 0, 0.0, pltpu.roll(tile, 1, 1))
        beside = beside + jnp.where(lanes == last, 0.0, pltpu.roll(tile, last, 1))
        if y > 0:
            beside = beside + field[l - 1]
        if y < plane - 1:
            beside = beside + field[l + 1]
        beside = beside + (field[l - plane] if l >= plane else before[l].astype(F32))
        beside = beside + (
            field[l + plane] if l + plane < tiles else after[l + plane - tiles].astype(F32)
        )
        out[l] = diagonal[l : l + 1, :] * tile - beside


def regularize_first(plane, field, before, after, diagonal, smooth, gram_own):
    smooth_field(field, before, after, diagonal, smooth, plane)
    gram_own[...] = gram(field, smooth)


def regularize_kernel(
    plane, field, before, after, diagonal, smooth_old, direction, solution, alpha,
    smooth, gram_own, gram_cross, solution_out,
):
    smooth_field(field, before, after, diagonal, smooth, plane)
    gram_own[...] = gram(field, smooth)
    gram_cross[...] = gram(field, smooth_old)
    spread = spread_mixing(alpha[...])
    for l in range(field.shape[0]):
        solution_out[l] = solution[l] + mix_tile(direction[l], spread)


def data_kernel(first, copies, slots, share, place, arrived, panels, row_weight, *refs):
    if first:
        gram_own, norm_out, response_out, gram_out, outgoing = refs
    else:
        (gram_own, gram_cross, gram_old, norm_old, response_old,
         norm_out, beta_out, response_out, gram_out, outgoing) = refs
    per = slots + 1
    tx_here, rows_here, width = panels.shape
    columns, block_len = arrived.shape[1:]
    foot_len = width // block_len
    total = arrived[slots].astype(F32)
    for m in range(1, copies):
        total = total + arrived[m * per + slots].astype(F32)
    norm = join_three(total)
    norm_out[...] = norm
    beta = None
    pair = gram_own[...]
    if not first:
        beta = solve_small(norm_old[...], norm)
        beta_out[...] = beta
        cross = small_dot(gram_cross[...], beta, ((1,), (0,)))
        inner = small_dot(gram_old[...], beta, ((1,), (0,)))
        pair = pair + cross + cross.T + small_dot(beta, inner, ((0,), (0,)))
    gram_out[...] = pair
    curvature = share * pair
    empty = jnp.zeros((columns, block_len), BF16)
    for m in range(copies):
        for s in range(slots):
            outgoing[m * per + s] = empty
    for t in range(tx_here):
        picked = jnp.concatenate([arrived[place[t, f]] for f in range(foot_len)], axis=1)
        response = nt(picked, panels[t])
        if not first:
            response = response + small_dot(beta, response_old[t], ((0,), (0,)))
        response_out[t] = response
        weighted = response * row_weight[t : t + 1, :]
        curvature = curvature + gram_halves(halves(response), halves(weighted))
        shares = jnp.dot(weighted.astype(BF16), panels[t], preferred_element_type=F32).astype(BF16)
        for f in range(foot_len):
            outgoing[place[t, f]] = shares[:, f * block_len : (f + 1) * block_len]
    pieces = split_three(curvature)
    for m in range(copies):
        outgoing[m * per + slots] = pieces


def mix_kernel(fresh, smooth_fresh, direction, smooth, beta, direction_out, smooth_out):
    spread = spread_mixing(beta[...])
    for l in range(fresh.shape[0]):
        direction_out[l] = fresh[l] + mix_tile(direction[l], spread)
        smooth_out[l] = smooth_fresh[l] + mix_tile(smooth[l], spread)


def sum_kernel(copies, slots, incoming, handed):
    per = slots + 1
    for s in range(per):
        total = incoming[s].astype(F32)
        for m in range(1, copies):
            total = total + incoming[m * per + s].astype(F32)
        handed[s] = total.astype(BF16) if s < slots else split_three(join_three(total))


def owners_ranks(tile_ids, blocks_dev):
    owners = tile_ids // blocks_dev
    position = jnp.arange(tile_ids.shape[1])
    before = (owners[:, :, None] == owners[:, None, :]) & (
        position[None, None, :] < position[None, :, None]
    )
    ranking = jnp.sum(before.astype(jnp.int32), axis=2)
    return (owners, tile_ids - owners * blocks_dev, ranking)


def shards(right_side, depth_weight, panels, data_weight, footprints, counts):
    columns, extent_x, extent_y, block_len = right_side.shape
    tx_here, rows_here, foot_len, _ = panels.shape
    copies = lax.axis_size("mod")
    src_count = lax.axis_size("src")
    tiles = extent_x * extent_y
    plane = extent_y
    slots = tx_here * CAP
    per = slots + 1
    mod_index = lax.axis_index("mod")
    src_index = lax.axis_index("src")
    group_counts = lax.dynamic_slice_in_dim(counts, src_index * tx_here, tx_here, 0)
    owners_all, within_all, ranking_all = owners_ranks(footprints, tiles)
    mine = lambda ids: lax.dynamic_slice_in_dim(ids, src_index * tx_here, tx_here, 0)
    place = mine(owners_all) * per + jnp.arange(tx_here)[:, None] * CAP + mine(ranking_all)
    chosen = (owners_all == mod_index)[:, None, :] & (
        ranking_all[:, None, :] == jnp.arange(CAP)[None, :, None]
    )
    slot_tile = jnp.min(jnp.where(chosen, within_all[:, None, :], tiles), axis=2)
    own_tile = jnp.minimum(mine(slot_tile).reshape(-1), tiles - 1)
    slot_tile = slot_tile.reshape(-1)
    row_ids = mod_index * rows_here + jnp.arange(rows_here)
    row_weight = data_weight * (row_ids[None, :] < group_counts[:, None]).astype(F32)
    up = [(i, i + 1) for i in range(copies - 1)]
    down = [(i + 1, i) for i in range(copies - 1)]
    flat_panels = panels.reshape(tx_here, rows_here, foot_len * block_len)
    diagonal = 6.0 + depth_weight.reshape(tiles, block_len)
    share = 1.0 / src_count

    field = ((tiles, columns, block_len), F32)
    small = ((columns, columns), F32)
    edge = ((plane, columns, block_len), BF16)
    packet = ((copies * per, columns, block_len), BF16)
    responses = ((tx_here, columns, rows_here), F32)
    image = pltpu.VMEM((tiles + 1, columns, block_len), F32)

    residual = right_side.transpose(1, 2, 0, 3).reshape(field[0])
    sent, first_plane, last_plane = call(
        functools.partial(begin_kernel, copies, slots, plane),
        [packet, edge, edge],
        (own_tile, residual),
        (SMEM, VMEM),
    )
    solution = jnp.zeros_like(residual)
    direction = smooth = norm = response = gram_pair = alpha = None
    for iteration in range(ITERS):
        first = iteration == 0
        arrived = lax.all_to_all(sent, "mod", 0, 0, tiled=True)
        before = lax.ppermute(last_plane, "mod", up)
        after = lax.ppermute(first_plane, "mod", down)
        if first:
            smooth, gram_own = call(
                functools.partial(regularize_first, plane),
                [field, small],
                (residual, before, after, diagonal),
                (VMEM,) * 4,
            )
            direction = residual
            norm, response, gram_pair, outgoing = call(
                functools.partial(data_kernel, True, copies, slots, share),
                [small, responses, small, packet],
                (place, arrived, flat_panels, row_weight, gram_own),
                (SMEM,) + (VMEM,) * 4,
            )
            incoming = lax.all_to_all(outgoing, "mod", 0, 0, tiled=True)
        else:
            smooth_fresh, gram_own, gram_cross, solution = call(
                functools.partial(regularize_kernel, plane),
                [field, small, small, field],
                (residual, before, after, diagonal, smooth, direction, solution, alpha),
                (VMEM,) * 8,
            )
            norm, beta, response, gram_pair, outgoing = call(
                functools.partial(data_kernel, False, copies, slots, share),
                [small, small, responses, small, packet],
                (place, arrived, flat_panels, row_weight, gram_own, gram_cross, gram_pair, norm,
                 response),
                (SMEM,) + (VMEM,) * 8,
            )
            incoming = lax.all_to_all(outgoing, "mod", 0, 0, tiled=True)
            direction, smooth = call(
                mix_kernel,
                [field, field],
                (residual, smooth_fresh, direction, smooth, beta),
                (VMEM,) * 5,
            )
        (handed,) = call(
            functools.partial(sum_kernel, copies, slots),
            [((per, columns, block_len), BF16)],
            (incoming,),
            (VMEM,),
        )
        groups = lax.all_gather(handed, "src", axis=0, tiled=True)
        if iteration + 1 < ITERS:
            residual, alpha, sent, first_plane, last_plane = call(
                functools.partial(step_kernel, src_count, copies, slots, plane),
                [field, small, packet, edge, edge],
                (slot_tile, own_tile, groups, residual, smooth, norm),
                (SMEM, SMEM) + (VMEM,) * 4,
                scratch=(image,),
            )
        else:
            residual, solution = call(
                functools.partial(last_kernel, src_count, slots),
                [field, field],
                (slot_tile, groups, residual, smooth, norm, direction, solution),
                (SMEM,) + (VMEM,) * 6,
                scratch=(image,),
            )

    def to_field(parts):
        return parts.reshape(extent_x, extent_y, columns, block_len).transpose(2, 0, 1, 3)

    return (to_field(solution), to_field(residual))


def solution(mesh):
    placed = (
        P(None, "mod", None, None),
        P("mod", None, None),
        P("src", "mod", None, None),
        P("src", "mod"),
        P(),
        P(),
    )
    return jax.shard_map(
        shards,
        mesh=mesh,
        in_specs=placed,
        out_specs=(P(None, "mod", None, None), P(None, "mod", None, None)),
        check_vma=False,
    )
```

time: 1780 us -> 351 us (0.20)
  waiting for transfers between devices: 1250 us -> 138 us
  blocking collectives: 353 us -> 72.4 us
  matrix products: 51.2 us -> 0 us
  starting transfers between devices: 12.9 us -> 62.2 us
  other arithmetic: 41.7 us -> 0.58 us
  Pallas kernels: 0 us -> 39.5 us
    reduce_scatter x3 -> x0, waiting for transfers between devices: 625 us -> none  [shards(): lax.psum_scatter(slotted.astype(jnp.bfloat16), 'mod', scatter_dimension=1...]
    psum x3 -> x0, waiting for transfers between devices: 353 us -> none  [shards(): lax.psum(own_terms.astype(jnp.bfloat16), 'src').astype(jnp.float32)]
    psum x5 -> x0, blocking collectives: 353 us -> none  [the longest x2 123 us: shards(): curvature = lax.psum(inner_block(direction, image), 'mod')]
    all_gather x3 -> x0, waiting for transfers between devices: 277 us -> none  [shards(): arrived = lax.all_gather(packed, 'mod', axis=1, tiled=True)]
    all_gather x0 -> x3, blocking collectives: none -> 72.4 us  [shards(): groups = lax.all_gather(handed, 'src', axis=0, tiled=True)]
    all_to_all x0 -> x6, waiting for transfers between devices: none -> 72.2 us  [the longest x3 72.2 us: shards(): incoming = lax.all_to_all(outgoing, 'mod', 0, 0, tiled=True)]
    ppermute x6, waiting for transfers between devices: 0.02 us -> 66.1 us  [the longest x3 56.1 us: shards(): before = lax.ppermute(last_plane, 'mod', up)]
    all_to_all x0 -> x6, starting transfers between devices: none -> 49.1 us  [the longest x3 28.4 us: shards(): incoming = lax.all_to_all(outgoing, 'mod', 0, 0, tiled=True)]
  transfers between devices with their start and end apart: 15 -> 12, of which waited for: 9 -> 9; matrix products, arithmetic and copies ran while one was open for 2% -> 1% of each run, Pallas kernels for 0% -> 2%
where the time goes in v1:
time: 351 us; the launch traced here: 350 us
  waiting for transfers between devices  138 us (39%)
  blocking collectives  72.4 us (21%)
  starting transfers between devices  62.2 us (18%)
  Pallas kernels  39.5 us (11%)
  local copies, waits for them, and re-layouts  35.6 us (10%)
    all_gather x3, blocking collectives, shards(): groups = lax.all_gather(handed, 'src', axis=0, tiled=True)  72.4 us
    all_to_all x3, waiting for transfers between devices, shards(): incoming = lax.all_to_all(outgoing, 'mod', 0, 0, tiled=True)  72.2 us
    ppermute x3, waiting for transfers between devices, shards(): before = lax.ppermute(last_plane, 'mod', up)  56.1 us
    pallas_call x15, Pallas kernels, call(): pl.pallas_call(kernel, out_shape=[jax.ShapeDtypeStruct(shape, dtype) for...  39.5 us
    all_to_all x3, starting transfers between devices, shards(): incoming = lax.all_to_all(outgoing, 'mod', 0, 0, tiled=True)  28.4 us
    unnamed x88, local copies, waits for them, and re-layouts  28 us
    all_to_all x3, starting transfers between devices, shards(): arrived = lax.all_to_all(sent, 'mod', 0, 0, tiled=True)  20.8 us
    ppermute x3, waiting for transfers between devices, shards(): after = lax.ppermute(first_plane, 'mod', down)  10 us
  transfers between devices with their start and end apart: 12, of which 9 were waited for; matrix products, arithmetic and copies ran while one was open for 1% of the time, Pallas kernels for 2%

profile of v1, /device:TPU:1, one launch (start us, length us, event | category | flops | bytes accessed | tf_op | source)
XLA Modules:
  0.0 349.6 jit_solution(14309315440575577178)
XLA Ops:
  0.7 0.8 copy.47
  2.3 1.4 copy.61
  3.6 2.1 shard_map.77
  5.7 0.8 copy-done
  6.5 10.7 %all-to-all-start = ((bf16[288,16,128]{2,1,0:T(8,128)(2,1)}), bf16[288,16,128]{2,1,0:T(8,128)(2,1)}, u32[]{:S(2)}, u32[]{:S(2)}) async-start(bf16[288,16,128]{2,1,0:T(8,128)(2,1)} %get-tuple-element.43), calls=%async_computation | async-start | bytes 2359296 | tf_op jit(solution)/shard_map/all_to_all | solution.py:311
  17.3 3.1 collective-permute-start
  20.4 1.3 collective-permute-start.1
  22.1 4.1 %reshape.57.panels = bf16[4,96,4096]{2,1,0:T(8,128)(2,1)S(1)} reshape(bf16[4,96,32,128]{3,2,1,0:T(8,128)(2,1)} %param.8) | data formatting | bytes 6291456 | tf_op jit(solution)/shard_map/reshape | solution.py:289
  26.2 15.0 %collective-permute-done.before = bf16[16,16,128]{2,1,0:T(8,128)(2,1)S(1)} collective-permute-done((bf16[16,16,128]{2,1,0:T(8,128)(2,1)S(1)}, bf16[16,16,128]{2,1,0:T(8,128)(2,1)S(1)}, u32[]{:S(2)}, u32[]{:S(2)}) %collective-permute-start) | collective-permute-done | bytes 65568 | tf_op jit(solution)/shard_map/ppermute | solution.py:312
  41.2 3.2 collective-permute-done.1.after
  44.4 1.0 copy-done.1
  46.0 0.8 copy-done.5
  46.8 4.3 %shard_map.79 = (f32[16,16]{1,0:T(8,128)S(1)}, f32[4,16,96]{2,1,0:T(8,128)S(1)}, f32[16,16]{1,0:T(8,128)S(1)}, bf16[288,16,128]{2,1,0:T(8,128)(2,1)S(1)}) custom-call(s32[4,32]{1,0:T(4,128)S(1)} %add_add_fusion.place, bf16[288,16,128]{2,1,0:T(8,128)(2,1)} %all-to-all-done.arrived, bf16[4,96,4096]{2,1,0:T(8,128)(2,1)S(1)} %reshape.57.panels, ...), custom_call_target="tpu_custom_call" | custom-call | tf_op jit(solution)/shard_map/pallas_call | solution.py:19
  51.1 1.0 copy-done.27
  52.1 10.0 %all-to-all-start.1 = ((bf16[288,16,128]{2,1,0:T(8,128)(2,1)}), bf16[288,16,128]{2,1,0:T(8,128)(2,1)}, u32[]{:S(2)}, u32[]{:S(2)}) async-start(bf16[288,16,128]{2,1,0:T(8,128)(2,1)} %copy-done.27), calls=%async_computation.1 | async-start | bytes 2359296 | tf_op jit(solution)/shard_map/all_to_all | solution.py:328
  62.3 27.3 %all-to-all-done.1.incoming = bf16[288,16,128]{2,1,0:T(8,128)(2,1)} async-done(((bf16[288,16,128]{2,1,0:T(8,128)(2,1)}), bf16[288,16,128]{2,1,0:T(8,128)(2,1)}, u32[]{:S(2)}, u32[]{:S(2)}) %all-to-all-start.1) | async-done | bytes 1179680 | tf_op jit(solution)/shard_map/all_to_all | solution.py:328
  89.6 1.6 shard_map.80
  91.2 29.4 %all_gather.9.groups = bf16[144,16,128]{2,1,0:T(8,128)(2,1)S(1)} all-gather(bf16[9,16,128]{2,1,0:T(8,128)(2,1)S(1)} %shard_map.80), channel_id=1, replica_groups=mesh['src'=16,'mod'=32] {'src'}, dimensions={0}, use_global_device_ids=true | all-gather | bytes 626688 | tf_op jit(solution)/shard_map/all_gather | solution.py:356
  120.6 3.8 %shard_map.81 = (f32[64,16,128]{2,1,0:T(8,128)S(1)}, f32[16,16]{1,0:T(8,128)S(1)}, bf16[288,16,128]{2,1,0:T(8,128)(2,1)S(1)}, bf16[16,16,128]{2,1,0:T(8,128)(2,1)S(1)}, bf16[16,16,128]{2,1,0:T(8,128)(2,1)S(1)}) custom-call(s32[128]{0:T(128)S(1)} %reshape.55.slot_tile, s32[8]{0:T(128)S(1)} %min.6.own_tile, bf16[144,16,128]{2,1,0:T(8,128)(2,1)S(1)} %all_gather.9.groups, ...), custom_call_target="tpu_custom_call" | custom-call | tf_op jit(solution)/shard_map/pallas_call | solution.py:19
  125.2 1.0 copy-done.24
  126.2 5.0 %all-to-all-start.2 = ((bf16[288,16,128]{2,1,0:T(8,128)(2,1)}), bf16[288,16,128]{2,1,0:T(8,128)(2,1)}, u32[]{:S(2)}, u32[]{:S(2)}) async-start(bf16[288,16,128]{2,1,0:T(8,128)(2,1)} %copy-done.24), calls=%async_computation.2 | async-start | bytes 2359296 | tf_op jit(solution)/shard_map/all_to_all | solution.py:311
  131.3 3.1 collective-permute-start.2
  134.3 1.3 collective-permute-start.3
  135.6 20.5 %collective-permute-done.2.before = bf16[16,16,128]{2,1,0:T(8,128)(2,1)S(1)} collective-permute-done((bf16[16,16,128]{2,1,0:T(8,128)(2,1)S(1)}, bf16[16,16,128]{2,1,0:T(8,128)(2,1)S(1)}, u32[]{:S(2)}, u32[]{:S(2)}) %collective-permute-start.2) | collective-permute-done | bytes 65568 | tf_op jit(solution)/shard_map/ppermute | solution.py:312
  156.2 3.4 collective-permute-done.3.after
  159.7 1.0 copy-done.3
  160.7 1.0 copy-done.7
  161.7 1.0 copy-done.17
  162.8 1.4 shard_map.82
  164.2 0.8 copy-done.28
  165.8 6.0 %shard_map.83 = (f32[16,16]{1,0:T(8,128)S(1)}, f32[16,16]{1,0:T(8,128)S(1)}, f32[4,16,96]{2,1,0:T(8,128)S(1)}, f32[16,16]{1,0:T(8,128)S(1)}, bf16[288,16,128]{2,1,0:T(8,128)(2,1)S(1)}) custom-call(s32[4,32]{1,0:T(4,128)S(1)} %add_add_fusion.place, bf16[288,16,128]{2,1,0:T(8,128)(2,1)} %all-to-all-done.2.arrived, bf16[4,96,4096]{2,1,0:T(8,128)(2,1)S(1)} %reshape.57.panels, ...), custom_call_target="tpu_custom_call" | custom-call | tf_op jit(solution)/shard_map/pallas_call | solution.py:19
  171.8 1.0 copy-done.26
  172.8 9.3 %all-to-all-start.3 = ((bf16[288,16,128]{2,1,0:T(8,128)(2,1)}), bf16[288,16,128]{2,1,0:T(8,128)(2,1)}, u32[]{:S(2)}, u32[]{:S(2)}) async-start(bf16[288,16,128]{2,1,0:T(8,128)(2,1)} %copy-done.26), calls=%async_computation.3 | async-start | bytes 2359296 | tf_op jit(solution)/shard_map/all_to_all | solution.py:343
  182.1 1.0 copy-done.4
  183.1 1.0 copy-done.8
  184.1 1.0 copy-done.18
  185.2 1.0 copy-done.35
  186.2 1.2 shard_map.85
  187.5 0.8 copy-done.9
  189.0 20.3 %all-to-all-done.3.incoming = bf16[288,16,128]{2,1,0:T(8,128)(2,1)} async-done(((bf16[288,16,128]{2,1,0:T(8,128)(2,1)}), bf16[288,16,128]{2,1,0:T(8,128)(2,1)}, u32[]{:S(2)}, u32[]{:S(2)}) %all-to-all-start.3) | async-done | bytes 1179680 | tf_op jit(solution)/shard_map/all_to_all | solution.py:343
  209.3 1.6 shard_map.84
  210.9 20.6 %all_gather.10.groups = bf16[144,16,128]{2,1,0:T(8,128)(2,1)S(1)} all-gather(bf16[9,16,128]{2,1,0:T(8,128)(2,1)S(1)} %shard_map.84), channel_id=1, replica_groups=mesh['src'=16,'mod'=32] {'src'}, dimensions={0}, use_global_device_ids=true | all-gather | bytes 626688 | tf_op jit(solution)/shard_map/all_gather | solution.py:356
  231.6 3.8 %shard_map.86 = (f32[64,16,128]{2,1,0:T(8,128)S(1)}, f32[16,16]{1,0:T(8,128)S(1)}, bf16[288,16,128]{2,1,0:T(8,128)(2,1)S(1)}, bf16[16,16,128]{2,1,0:T(8,128)(2,1)S(1)}, bf16[16,16,128]{2,1,0:T(8,128)(2,1)S(1)}) custom-call(s32[128]{0:T(128)S(1)} %reshape.55.slot_tile, s32[8]{0:T(128)S(1)} %min.6.own_tile, bf16[144,16,128]{2,1,0:T(8,128)(2,1)S(1)} %all_gather.10.groups, ...), custom_call_target="tpu_custom_call" | custom-call | tf_op jit(solution)/shard_map/pallas_call | solution.py:19
  236.2 1.0 copy-done.23
  237.2 5.0 %all-to-all-start.4 = ((bf16[288,16,128]{2,1,0:T(8,128)(2,1)}), bf16[288,16,128]{2,1,0:T(8,128)(2,1)}, u32[]{:S(2)}, u32[]{:S(2)}) async-start(bf16[288,16,128]{2,1,0:T(8,128)(2,1)} %copy-done.23), calls=%async_computation.4 | async-start | bytes 2359296 | tf_op jit(solution)/shard_map/all_to_all | solution.py:311
  242.2 3.1 collective-permute-start.4
  245.3 1.3 collective-permute-start.5
  246.6 20.5 %collective-permute-done.4.before = bf16[16,16,128]{2,1,0:T(8,128)(2,1)S(1)} collective-permute-done((bf16[16,16,128]{2,1,0:T(8,128)(2,1)S(1)}, bf16[16,16,128]{2,1,0:T(8,128)(2,1)S(1)}, u32[]{:S(2)}, u32[]{:S(2)}) %collective-permute-start.4) | collective-permute-done | bytes 65568 | tf_op jit(solution)/shard_map/ppermute | solution.py:312
  267.2 3.4 collective-permute-done.5.after
  270.6 1.0 copy-done.11
  271.6 1.0 copy-done.14
  272.7 1.0 copy-done.21
  273.7 1.0 copy-done.29
  274.8 1.4 shard_map.87
  276.9 0.8 copy-done.32
  277.7 6.5 %shard_map.88 = (f32[16,16]{1,0:T(8,128)S(1)}, f32[16,16]{1,0:T(8,128)S(1)}, f32[4,16,96]{2,1,0:T(8,128)}, f32[16,16]{1,0:T(8,128)}, bf16[288,16,128]{2,1,0:T(8,128)(2,1)S(1)}) custom-call(s32[4,32]{1,0:T(4,128)S(1)} %add_add_fusion.place, bf16[288,16,128]{2,1,0:T(8,128)(2,1)} %all-to-all-done.4.arrived, bf16[4,96,4096]{2,1,0:T(8,128)(2,1)S(1)} %reshape.57.panels, ...), custom_call_target="tpu_custom_call" | custom-call | tf_op jit(solution)/shard_map/pallas_call | solution.py:19
  284.2 1.0 copy-done.25
  285.3 9.1 %all-to-all-start.5 = ((bf16[288,16,128]{2,1,0:T(8,128)(2,1)}), bf16[288,16,128]{2,1,0:T(8,128)(2,1)S(1)}, u32[]{:S(2)}, u32[]{:S(2)}) async-start(bf16[288,16,128]{2,1,0:T(8,128)(2,1)} %copy-done.25), calls=%async_computation.5 | async-start | bytes 2359296 | tf_op jit(solution)/shard_map/all_to_all | solution.py:343
  294.5 1.2 shard_map.90
  296.5 0.8 copy-done.38
  297.3 24.6 %all-to-all-done.5.incoming = bf16[288,16,128]{2,1,0:T(8,128)(2,1)S(1)} async-done(((bf16[288,16,128]{2,1,0:T(8,128)(2,1)}), bf16[288,16,128]{2,1,0:T(8,128)(2,1)S(1)}, u32[]{:S(2)}, u32[]{:S(2)}) %all-to-all-start.5) | async-done | bytes 1179680 | tf_op jit(solution)/shard_map/all_to_all | solution.py:343
  322.1 22.4 %all_gather.11.groups = bf16[144,16,128]{2,1,0:T(8,128)(2,1)S(1)} all-gather(bf16[9,16,128]{2,1,0:T(8,128)(2,1)S(1)} %shard_map.89), channel_id=1, replica_groups=mesh['src'=16,'mod'=32] {'src'}, dimensions={0}, use_global_device_ids=true | all-gather | bytes 626688 | tf_op jit(solution)/shard_map/all_gather | solution.py:356
  344.5 3.8 %shard_map.91 = (f32[64,16,128]{2,1,0:T(8,128)S(1)}, f32[64,16,128]{2,1,0:T(8,128)S(1)}) custom-call(s32[128]{0:T(128)S(1)} %reshape.55.slot_tile, bf16[144,16,128]{2,1,0:T(8,128)(2,1)S(1)} %all_gather.11.groups, f32[64,16,128]{2,1,0:T(8,128)S(1)} %copy-done.15, f32[64,16,128]{2,1,0:T(8,128)S(1)} %copy-done.39, f32[16,16]{1,0:T(8,128)S(1)} %get-tuple-element.79.norm, ...), custom_call_target="tpu_custom_call" | custom-call | tf_op jit(solution)/shard_map/pallas_call | solution.py:19
  348.3 1.3 copy_bitcast_fusion
  (90 shorter events, 7.1 us)
Async XLA Ops:
  5.7 0.8 copy-start
  6.5 15.1 %copy-start.42 = (s32[64]{0:T(128)S(1)}, s32[64]{0:T(128)}, u32[]{:S(2)}) copy-start(s32[64]{0:T(128)} %param.11) | copy-start | bytes 772
  6.5 15.4 %copy-start.41 = (f32[4,96]{1,0:T(4,128)S(1)}, f32[4,96]{1,0:T(4,128)}, u32[]{:S(2)}) copy-start(f32[4,96]{1,0:T(4,128)} %param.9) | copy-start | bytes 4612
  6.5 15.5 %copy-start.40 = (f32[4,16,128]{2,1,0:T(8,128)S(1)}, f32[4,16,128]{2,1,0:T(8,128)}, u32[]{:S(2)}) copy-start(f32[4,16,128]{2,1,0:T(8,128)} %param.7) | copy-start | bytes 98308
  6.5 40.2 %all-to-all-start = ((bf16[288,16,128]{2,1,0:T(8,128)(2,1)}), bf16[288,16,128]{2,1,0:T(8,128)(2,1)}, u32[]{:S(2)}, u32[]{:S(2)}) async-start(bf16[288,16,128]{2,1,0:T(8,128)(2,1)} %get-tuple-element.43), calls=%async_computation | async-start | bytes 2359296 | tf_op jit(solution)/shard_map/all_to_all | solution.py:311
  17.3 23.9 %collective-permute-start = (bf16[16,16,128]{2,1,0:T(8,128)(2,1)S(1)}, bf16[16,16,128]{2,1,0:T(8,128)(2,1)S(1)}, u32[]{:S(2)}, u32[]{:S(2)}) collective-permute-start(bf16[16,16,128]{2,1,0:T(8,128)(2,1)S(1)} %get-tuple-element.44), channel_id=1, source_target_pairs={{0,1},{1,2},{2,3},{3,4},{4,5},{5,6},{6,7},{7,8},{8,9},{9,10},{10,1... | collective-permute-start | bytes 196616 | tf_op jit(solution)/shard_map/ppermute | solution.py:312
  20.4 24.0 %collective-permute-start.1 = (bf16[16,16,128]{2,1,0:T(8,128)(2,1)S(1)}, bf16[16,16,128]{2,1,0:T(8,128)(2,1)S(1)}, u32[]{:S(2)}, u32[]{:S(2)}) collective-permute-start(bf16[16,16,128]{2,1,0:T(8,128)(2,1)S(1)} %get-tuple-element.45), channel_id=1, source_target_pairs={{1,0},{2,1},{3,2},{4,3},{5,4},{6,5},{7,6},{8,7},{9,8},{10,9},{11,1... | collective-permute-start | bytes 196616 | tf_op jit(solution)/shard_map/ppermute | solution.py:313
  44.4 1.0 copy-start.1
  46.0 0.8 copy-start.5
  51.1 1.0 copy-start.27
  52.1 37.5 %all-to-all-start.1 = ((bf16[288,16,128]{2,1,0:T(8,128)(2,1)}), bf16[288,16,128]{2,1,0:T(8,128)(2,1)}, u32[]{:S(2)}, u32[]{:S(2)}) async-start(bf16[288,16,128]{2,1,0:T(8,128)(2,1)} %copy-done.27), calls=%async_computation.1 | async-start | bytes 2359296 | tf_op jit(solution)/shard_map/all_to_all | solution.py:328
  89.6 31.0 %copy-start.2 = (f32[4,16,16,128]{3,2,1,0:T(8,128)S(1)}, f32[4,16,16,128]{3,2,1,0:T(8,128)}, u32[]{:S(2)}) copy-start(f32[4,16,16,128]{3,2,1,0:T(8,128)} %copy-done) | copy-start | bytes 1572868
  89.6 31.0 %copy-start.6 = (f32[64,16,128]{2,1,0:T(8,128)S(1)}, f32[64,16,128]{2,1,0:T(8,128)}, u32[]{:S(2)}) copy-start(f32[64,16,128]{2,1,0:T(8,128)} %copy-done.5) | copy-start | bytes 1572868
  124.4 0.8 copy-start.16
  125.2 1.0 copy-start.24
  126.2 39.5 %all-to-all-start.2 = ((bf16[288,16,128]{2,1,0:T(8,128)(2,1)}), bf16[288,16,128]{2,1,0:T(8,128)(2,1)}, u32[]{:S(2)}, u32[]{:S(2)}) async-start(bf16[288,16,128]{2,1,0:T(8,128)(2,1)} %copy-done.24), calls=%async_computation.2 | async-start | bytes 2359296 | tf_op jit(solution)/shard_map/all_to_all | solution.py:311
  131.3 24.9 %collective-permute-start.2 = (bf16[16,16,128]{2,1,0:T(8,128)(2,1)S(1)}, bf16[16,16,128]{2,1,0:T(8,128)(2,1)S(1)}, u32[]{:S(2)}, u32[]{:S(2)}) collective-permute-start(bf16[16,16,128]{2,1,0:T(8,128)(2,1)S(1)} %get-tuple-element.52), channel_id=1, source_target_pairs={{0,1},{1,2},{2,3},{3,4},{4,5},{5,6},{6,7},{7,8},{8,9},{9,10},{10,1... | collective-permute-start | bytes 196616 | tf_op jit(solution)/shard_map/ppermute | solution.py:312
  134.3 25.3 %collective-permute-start.3 = (bf16[16,16,128]{2,1,0:T(8,128)(2,1)S(1)}, bf16[16,16,128]{2,1,0:T(8,128)(2,1)S(1)}, u32[]{:S(2)}, u32[]{:S(2)}) collective-permute-start(bf16[16,16,128]{2,1,0:T(8,128)(2,1)S(1)} %get-tuple-element.53), channel_id=1, source_target_pairs={{1,0},{2,1},{3,2},{4,3},{5,4},{6,5},{7,6},{8,7},{9,8},{10,9},{11,1... | collective-permute-start | bytes 196616 | tf_op jit(solution)/shard_map/ppermute | solution.py:313
  159.6 1.0 copy-start.3
  160.7 1.0 copy-start.7
  161.7 1.0 copy-start.17
  164.2 0.8 copy-start.28
  165.0 0.8 copy-start.34
  171.8 1.0 copy-start.26
  172.8 36.5 %all-to-all-start.3 = ((bf16[288,16,128]{2,1,0:T(8,128)(2,1)}), bf16[288,16,128]{2,1,0:T(8,128)(2,1)}, u32[]{:S(2)}, u32[]{:S(2)}) async-start(bf16[288,16,128]{2,1,0:T(8,128)(2,1)} %copy-done.26), calls=%async_computation.3 | async-start | bytes 2359296 | tf_op jit(solution)/shard_map/all_to_all | solution.py:343
  182.0 1.0 copy-start.4
  183.1 1.0 copy-start.8
  184.1 1.0 copy-start.18
  185.2 1.0 copy-start.35
  187.5 0.8 copy-start.9
  188.3 0.8 copy-start.20
  209.3 22.2 %copy-start.10 = (f32[64,16,128]{2,1,0:T(8,128)S(1)}, f32[64,16,128]{2,1,0:T(8,128)}, u32[]{:S(2)}) copy-start(f32[64,16,128]{2,1,0:T(8,128)} %copy-done.9) | copy-start | bytes 1572868
  209.3 22.2 %copy-start.19 = (f32[64,16,128]{2,1,0:T(8,128)S(1)}, f32[64,16,128]{2,1,0:T(8,128)}, u32[]{:S(2)}) copy-start(f32[64,16,128]{2,1,0:T(8,128)} %copy-done.16) | copy-start | bytes 1572868
  235.4 0.8 copy-start.13
  236.2 1.0 copy-start.23
  237.2 40.6 %all-to-all-start.4 = ((bf16[288,16,128]{2,1,0:T(8,128)(2,1)}), bf16[288,16,128]{2,1,0:T(8,128)(2,1)}, u32[]{:S(2)}, u32[]{:S(2)}) async-start(bf16[288,16,128]{2,1,0:T(8,128)(2,1)} %copy-done.23), calls=%async_computation.4 | async-start | bytes 2359296 | tf_op jit(solution)/shard_map/all_to_all | solution.py:311
  242.2 24.9 %collective-permute-start.4 = (bf16[16,16,128]{2,1,0:T(8,128)(2,1)S(1)}, bf16[16,16,128]{2,1,0:T(8,128)(2,1)S(1)}, u32[]{:S(2)}, u32[]{:S(2)}) collective-permute-start(bf16[16,16,128]{2,1,0:T(8,128)(2,1)S(1)} %get-tuple-element.66), channel_id=1, source_target_pairs={{0,1},{1,2},{2,3},{3,4},{4,5},{5,6},{6,7},{7,8},{8,9},{9,10},{10,1... | collective-permute-start | bytes 196616 | tf_op jit(solution)/shard_map/ppermute | solution.py:312
  245.3 25.3 %collective-permute-start.5 = (bf16[16,16,128]{2,1,0:T(8,128)(2,1)S(1)}, bf16[16,16,128]{2,1,0:T(8,128)(2,1)S(1)}, u32[]{:S(2)}, u32[]{:S(2)}) collective-permute-start(bf16[16,16,128]{2,1,0:T(8,128)(2,1)S(1)} %get-tuple-element.67), channel_id=1, source_target_pairs={{1,0},{2,1},{3,2},{4,3},{5,4},{6,5},{7,6},{8,7},{9,8},{10,9},{11,1... | collective-permute-start | bytes 196616 | tf_op jit(solution)/shard_map/ppermute | solution.py:313
  270.6 1.0 copy-start.11
  271.6 1.0 copy-start.14
  272.7 1.0 copy-start.21
  273.7 1.0 copy-start.29
  276.1 0.8 copy-start.30
  276.9 0.8 copy-start.32
  284.2 1.1 copy-start.25
  285.3 9.1 %copy-start.12 = (f32[64,16,128]{2,1,0:T(8,128)S(1)}, f32[64,16,128]{2,1,0:T(8,128)}, u32[]{:S(2)}) copy-start(f32[64,16,128]{2,1,0:T(8,128)} %copy-done.9) | copy-start | bytes 1572868
  285.3 9.1 %copy-start.15 = (f32[64,16,128]{2,1,0:T(8,128)S(1)}, f32[64,16,128]{2,1,0:T(8,128)}, u32[]{:S(2)}) copy-start(f32[64,16,128]{2,1,0:T(8,128)} %copy-done.13) | copy-start | bytes 1572868
  285.3 9.2 %copy-start.22 = (f32[64,16,128]{2,1,0:T(8,128)S(1)}, f32[64,16,128]{2,1,0:T(8,128)}, u32[]{:S(2)}) copy-start(f32[64,16,128]{2,1,0:T(8,128)} %copy-done.20) | copy-start | bytes 1572868
  285.3 9.2 %copy-start.33 = (f32[64,16,128]{2,1,0:T(8,128)S(1)}, f32[64,16,128]{2,1,0:T(8,128)}, u32[]{:S(2)}) copy-start(f32[64,16,128]{2,1,0:T(8,128)} %copy-done.32) | copy-start | bytes 1572868
  285.3 36.6 %all-to-all-start.5 = ((bf16[288,16,128]{2,1,0:T(8,128)(2,1)}), bf16[288,16,128]{2,1,0:T(8,128)(2,1)S(1)}, u32[]{:S(2)}, u32[]{:S(2)}) async-start(bf16[288,16,128]{2,1,0:T(8,128)(2,1)} %copy-done.25), calls=%async_computation.5 | async-start | bytes 2359296 | tf_op jit(solution)/shard_map/all_to_all | solution.py:343
  295.7 0.8 copy-start.36
  296.5 0.8 copy-start.38
  297.3 47.2 %copy-start.31 = (f32[64,16,128]{2,1,0:T(8,128)S(1)}, f32[64,16,128]{2,1,0:T(8,128)}, u32[]{:S(2)}) copy-start(f32[64,16,128]{2,1,0:T(8,128)} %copy-done.30) | copy-start | bytes 1572868
  321.9 22.6 %copy-start.37 = (f32[64,16,128]{2,1,0:T(8,128)S(1)}, f32[64,16,128]{2,1,0:T(8,128)}, u32[]{:S(2)}) copy-start(f32[64,16,128]{2,1,0:T(8,128)} %copy-done.36) | copy-start | bytes 1572868
  321.9 22.6 %copy-start.39 = (f32[64,16,128]{2,1,0:T(8,128)S(1)}, f32[64,16,128]{2,1,0:T(8,128)}, u32[]{:S(2)}) copy-start(f32[64,16,128]{2,1,0:T(8,128)} %copy-done.38) | copy-start | bytes 1572868

commit v2 on v1

--- a/solution.py
+++ b/solution.py
@@ -8,6 +8,7 @@
 from jax.sharding import PartitionSpec as P
 
 CAP = 2
+INNER = 8
 ITERS = 3
 F32 = jnp.float32
 BF16 = jnp.bfloat16
@@ -242,13 +243,13 @@
         smooth_out[l] = smooth_fresh[l] + mix_tile(smooth[l], spread)
 
 
-def sum_kernel(copies, slots, incoming, handed):
+def sum_kernel(copies, blocks, slots, incoming, handed):
     per = slots + 1
-    for s in range(per):
+    for s in range(blocks * per):
         total = incoming[s].astype(F32)
         for m in range(1, copies):
-            total = total + incoming[m * per + s].astype(F32)
-        handed[s] = total.astype(BF16) if s < slots else split_three(join_three(total))
+            total = total + incoming[m * blocks * per + s].astype(F32)
+        handed[s] = total.astype(BF16) if s % per < slots else split_three(join_three(total))
 
 
 def owners_ranks(tile_ids, blocks_dev):
@@ -289,18 +290,33 @@
     flat_panels = panels.reshape(tx_here, rows_here, foot_len * block_len)
     diagonal = 6.0 + depth_weight.reshape(tiles, block_len)
     share = 1.0 / src_count
+    inner = INNER
+    across_x = copies // inner
+    along_y = [[x * inner + y for y in range(inner)] for x in range(across_x)]
+    along_x = [[x * inner + y for x in range(across_x)] for y in range(inner)]
 
     field = ((tiles, columns, block_len), F32)
     small = ((columns, columns), F32)
     edge = ((plane, columns, block_len), BF16)
     packet = ((copies * per, columns, block_len), BF16)
+    part = ((inner * per, columns, block_len), BF16)
+
+    def reduced(outgoing):
+        halfway = lax.all_to_all(
+            outgoing, "mod", 0, 0, tiled=True, axis_index_groups=along_x
+        )
+        (halfway,) = call(
+            functools.partial(sum_kernel, across_x, inner, slots), [part], (halfway,), (VMEM,)
+        )
+        return lax.all_to_all(halfway, "mod", 0, 0, tiled=True, axis_index_groups=along_y)
+
     responses = ((tx_here, columns, rows_here), F32)
     image = pltpu.VMEM((tiles + 1, columns, block_len), F32)
 
     residual = right_side.transpose(1, 2, 0, 3).reshape(field[0])
     sent, first_plane, last_plane = call(
-        functools.partial(begin_kernel, copies, slots, plane),
-        [packet, edge, edge],
+        functools.partial(begin_kernel, inner, slots, plane),
+        [part, edge, edge],
         (own_tile, residual),
         (SMEM, VMEM),
     )
@@ -308,7 +324,11 @@
     direction = smooth = norm = response = gram_pair = alpha = None
     for iteration in range(ITERS):
         first = iteration == 0
-        arrived = lax.all_to_all(sent, "mod", 0, 0, tiled=True)
+        across = lax.all_to_all(sent, "mod", 0, 0, tiled=True, axis_index_groups=along_y)
+        across = jnp.broadcast_to(across[None], (across_x,) + across.shape)
+        arrived = lax.all_to_all(
+            across.reshape(packet[0]), "mod", 0, 0, tiled=True, axis_index_groups=along_x
+        )
         before = lax.ppermute(last_plane, "mod", up)
         after = lax.ppermute(first_plane, "mod", down)
         if first:
@@ -325,7 +345,7 @@
                 (place, arrived, flat_panels, row_weight, gram_own),
                 (SMEM,) + (VMEM,) * 4,
             )
-            incoming = lax.all_to_all(outgoing, "mod", 0, 0, tiled=True)
+            incoming = reduced(outgoing)
         else:
             smooth_fresh, gram_own, gram_cross, solution = call(
                 functools.partial(regularize_kernel, plane),
@@ -340,7 +360,7 @@
                  response),
                 (SMEM,) + (VMEM,) * 8,
             )
-            incoming = lax.all_to_all(outgoing, "mod", 0, 0, tiled=True)
+            incoming = reduced(outgoing)
             direction, smooth = call(
                 mix_kernel,
                 [field, field],
@@ -348,7 +368,7 @@
                 (VMEM,) * 5,
             )
         (handed,) = call(
-            functools.partial(sum_kernel, copies, slots),
+            functools.partial(sum_kernel, inner, 1, slots),
             [((per, columns, block_len), BF16)],
             (incoming,),
             (VMEM,),
@@ -356,8 +376,8 @@
         groups = lax.all_gather(handed, "src", axis=0, tiled=True)
         if iteration + 1 < ITERS:
             residual, alpha, sent, first_plane, last_plane = call(
-                functools.partial(step_kernel, src_count, copies, slots, plane),
-                [field, small, packet, edge, edge],
+                functools.partial(step_kernel, src_count, inner, slots, plane),
+                [field, small, part, edge, edge],
                 (slot_tile, own_tile, groups, residual, smooth, norm),
                 (SMEM, SMEM) + (VMEM,) * 4,
                 scratch=(image,),

time: 351 us -> 325 us (0.926)
  waiting for transfers between devices: 138 us -> 44.1 us
  blocking collectives: 72.4 us -> 154 us
  starting transfers between devices: 62.2 us -> 45.8 us
    all_to_all x0 -> x5, blocking collectives: none -> 80 us  [the longest x3 48.5 us: reduced(): lax.all_to_all(outgoing, 'mod', 0, 0, tiled=True, axis_index_groups=along_x)]
    ppermute x3, waiting for transfers between devices: 56.1 us -> 0.02 us  [shards(): before = lax.ppermute(last_plane, 'mod', up)]
    all_to_all x6 -> x7, waiting for transfers between devices: 72.2 us -> 35.9 us  [the longest x3 17.8 us: reduced(): lax.all_to_all(halfway, 'mod', 0, 0, tiled=True, axis_index_groups=along_y)]
    all_to_all x6 -> x7, starting transfers between devices: 49.1 us -> 35 us  [the longest x3 14 us: shards(): lax.all_to_all(across.reshape(packet[0]), 'mod', 0, 0, tiled=True, axis_i...]
    broadcast_in_dim x0 -> x3, local copies, waits for them, and re-layouts: none -> 3.53 us  [shards(): across = jnp.broadcast_to(across[None], (across_x,) + across.shape)]
    pallas_call x15 -> x18, Pallas kernels: 39.5 us -> 37.7 us  [call(): pl.pallas_call(kernel, out_shape=[jax.ShapeDtypeStruct(shape, dtype) for...]
    unnamed x88 -> x108, local copies, waits for them, and re-layouts: 28 us -> 26.5 us
  transfers between devices with their start and end apart: 12 -> 13, of which waited for: 9 -> 9; matrix products, arithmetic and copies ran while one was open for 1% -> 2% of each run, Pallas kernels for 2% -> 2%
where the time goes in v2:
time: 325 us; the launch traced here: 322 us
  blocking collectives  154 us (47%)
  starting transfers between devices  45.8 us (14%)
  waiting for transfers between devices  44.1 us (14%)
  local copies, waits for them, and re-layouts  38.9 us (12%)
  Pallas kernels  37.7 us (12%)
    all_gather x3, blocking collectives, shards(): groups = lax.all_gather(handed, 'src', axis=0, tiled=True)  74 us
    all_to_all x3, blocking collectives, reduced(): lax.all_to_all(outgoing, 'mod', 0, 0, tiled=True, axis_index_groups=along_x)  48.5 us
    pallas_call x18, Pallas kernels, call(): pl.pallas_call(kernel, out_shape=[jax.ShapeDtypeStruct(shape, dtype) for...  37.7 us
    all_to_all x2, blocking collectives, shards(): lax.all_to_all(sent, 'mod', 0, 0, tiled=True, axis_index_groups=along_y)  31.5 us
    unnamed x108, local copies, waits for them, and re-layouts  26.5 us
    all_to_all x3, waiting for transfers between devices, reduced(): lax.all_to_all(halfway, 'mod', 0, 0, tiled=True, axis_index_groups=along_y)  17.8 us
    all_to_all x3, starting transfers between devices, shards(): lax.all_to_all(across.reshape(packet[0]), 'mod', 0, 0, tiled=True, axis_i...  14 us
    all_to_all x3, starting transfers between devices, reduced(): lax.all_to_all(halfway, 'mod', 0, 0, tiled=True, axis_index_groups=along_y)  13.3 us
  transfers between devices with their start and end apart: 13, of which 9 were waited for; matrix products, arithmetic and copies ran while one was open for 2% of the time, Pallas kernels for 2%

profile of v2, /device:TPU:1, one launch (start us, length us, event | category | flops | bytes accessed | tf_op | source)
XLA Modules:
  0.0 322.3 jit_solution(5157816045406751002)
XLA Ops:
  2.3 1.4 copy.61
  3.7 1.8 shard_map.77
  6.2 7.6 %all-to-all-start = ((bf16[72,16,128]{2,1,0:T(8,128)(2,1)}), bf16[72,16,128]{2,1,0:T(8,128)(2,1)S(1)}, u32[]{:S(2)}, u32[]{:S(2)}) async-start(bf16[72,16,128]{2,1,0:T(8,128)(2,1)} %get-tuple-element.43), calls=%async_computation | async-start | bytes 589824 | tf_op jit(solution)/shard_map/all_to_all | solution.py:327
  13.9 3.4 %collective-permute-start = (bf16[16,16,128]{2,1,0:T(8,128)(2,1)S(1)}, bf16[16,16,128]{2,1,0:T(8,128)(2,1)S(1)}, u32[]{:S(2)}, u32[]{:S(2)}) collective-permute-start(bf16[16,16,128]{2,1,0:T(8,128)(2,1)S(1)} %get-tuple-element.44), channel_id=1, source_target_pairs={{0,1},{1,2},{2,3},{3,4},{4,5},{5,6},{6,7},{7,8},{8,9},{9,10},{10,1... | collective-permute-start | bytes 196616 | tf_op jit(solution)/shard_map/ppermute | solution.py:332
  17.3 1.3 collective-permute-start.1
  18.8 5.0 %all-to-all-done = bf16[72,16,128]{2,1,0:T(8,128)(2,1)S(1)} async-done(((bf16[72,16,128]{2,1,0:T(8,128)(2,1)}), bf16[72,16,128]{2,1,0:T(8,128)(2,1)S(1)}, u32[]{:S(2)}, u32[]{:S(2)}) %all-to-all-start) | async-done | bytes 294944 | tf_op jit(solution)/shard_map/all_to_all | solution.py:327
  23.8 1.2 broadcast_in_dim.22
  25.0 5.5 %all-to-all-start.1 = ((bf16[288,16,128]{2,1,0:T(8,128)(2,1)}), bf16[288,16,128]{2,1,0:T(8,128)(2,1)}, u32[]{:S(2)}, u32[]{:S(2)}) async-start(bf16[288,16,128]{2,1,0:T(8,128)(2,1)} %bitcast.2), calls=%async_computation.1 | async-start | bytes 2359296 | tf_op jit(solution)/shard_map/all_to_all | solution.py:329
  30.6 4.1 %reshape.70.panels = bf16[4,96,4096]{2,1,0:T(8,128)(2,1)S(1)} reshape(bf16[4,96,32,128]{3,2,1,0:T(8,128)(2,1)} %param.8) | data formatting | bytes 6291456 | tf_op jit(solution)/shard_map/reshape | solution.py:290
  34.8 1.0 copy-done.1
  37.2 6.3 %all-to-all-done.1.arrived = bf16[288,16,128]{2,1,0:T(8,128)(2,1)} async-done(((bf16[288,16,128]{2,1,0:T(8,128)(2,1)}), bf16[288,16,128]{2,1,0:T(8,128)(2,1)}, u32[]{:S(2)}, u32[]{:S(2)}) %all-to-all-start.1) | async-done | bytes 1179680 | tf_op jit(solution)/shard_map/all_to_all | solution.py:329
  43.5 4.3 %shard_map.79 = (f32[16,16]{1,0:T(8,128)S(1)}, f32[4,16,96]{2,1,0:T(8,128)S(1)}, f32[16,16]{1,0:T(8,128)S(1)}, bf16[288,16,128]{2,1,0:T(8,128)(2,1)S(1)}) custom-call(s32[4,32]{1,0:T(4,128)S(1)} %add_add_fusion.place, bf16[288,16,128]{2,1,0:T(8,128)(2,1)} %all-to-all-done.1.arrived, bf16[4,96,4096]{2,1,0:T(8,128)(2,1)S(1)} %reshape.70.panels, ...), custom_call_target="tpu_custom_call" | custom-call | tf_op jit(solution)/shard_map/pallas_call | solution.py:20
  47.8 14.4 %all_to_all.60.incoming = bf16[288,16,128]{2,1,0:T(8,128)(2,1)S(1)} all-to-all(bf16[288,16,128]{2,1,0:T(8,128)(2,1)S(1)} %get-tuple-element.47), channel_id=1, replica_groups={{0,8,16,24},{1,9,17,25},{2,10,18,26},{3,11,19,27},{4,12,20,28},{5,13,21..., dimensions={0} | all-to-all | bytes 2359296 | tf_op jit(solution)/shard_map/all_to_all | solution.py:305
  63.2 5.5 %all-to-all-start.3 = ((bf16[72,16,128]{2,1,0:T(8,128)(2,1)}), bf16[72,16,128]{2,1,0:T(8,128)(2,1)S(1)}, u32[]{:S(2)}, u32[]{:S(2)}) async-start(bf16[72,16,128]{2,1,0:T(8,128)(2,1)} %copy-done.24), calls=%async_computation.3 | async-start | bytes 589824 | tf_op jit(solution)/shard_map/all_to_all | solution.py:311
  69.5 0.9 reshape.67.slot_tile
  70.4 8.1 %all-to-all-done.3.incoming = bf16[72,16,128]{2,1,0:T(8,128)(2,1)S(1)} async-done(((bf16[72,16,128]{2,1,0:T(8,128)(2,1)}), bf16[72,16,128]{2,1,0:T(8,128)(2,1)S(1)}, u32[]{:S(2)}, u32[]{:S(2)}) %all-to-all-start.3) | async-done | bytes 294944 | tf_op jit(solution)/shard_map/all_to_all | solution.py:311
  78.7 30.6 %all_gather.9.groups = bf16[144,16,128]{2,1,0:T(8,128)(2,1)S(1)} all-gather(bf16[9,16,128]{2,1,0:T(8,128)(2,1)S(1)} %shard_map.81), channel_id=1, replica_groups=mesh['src'=16,'mod'=32] {'src'}, dimensions={0}, use_global_device_ids=true | all-gather | bytes 626688 | tf_op jit(solution)/shard_map/all_gather | solution.py:376
  109.3 1.0 copy-done.6
  110.3 3.7 %shard_map.82 = (f32[64,16,128]{2,1,0:T(8,128)S(1)}, f32[16,16]{1,0:T(8,128)S(1)}, bf16[72,16,128]{2,1,0:T(8,128)(2,1)S(1)}, bf16[16,16,128]{2,1,0:T(8,128)(2,1)S(1)}, bf16[16,16,128]{2,1,0:T(8,128)(2,1)S(1)}) custom-call(s32[128]{0:T(128)S(1)} %reshape.67.slot_tile, s32[8]{0:T(128)S(1)} %min.6.own_tile, bf16[144,16,128]{2,1,0:T(8,128)(2,1)S(1)} %all_gather.9.groups, ...), custom_call_target="tpu_custom_call" | custom-call | tf_op jit(solution)/shard_map/pallas_call | solution.py:20
  114.9 15.1 %all_to_all.61 = bf16[72,16,128]{2,1,0:T(8,128)(2,1)S(1)} all-to-all(bf16[72,16,128]{2,1,0:T(8,128)(2,1)S(1)} %get-tuple-element.50), channel_id=1, replica_groups={{0,1,2,3,4,5,6,7},{8,9,10,11,12,13,14,15},{16,17,18,19,20,21,22,23},{24..., dimensions={0} | all-to-all | bytes 589824 | tf_op jit(solution)/shard_map/all_to_all | solution.py:327
  129.9 1.2 broadcast_in_dim.23
  131.1 4.3 %all-to-all-start.5 = ((bf16[288,16,128]{2,1,0:T(8,128)(2,1)}), bf16[288,16,128]{2,1,0:T(8,128)(2,1)}, u32[]{:S(2)}, u32[]{:S(2)}) async-start(bf16[288,16,128]{2,1,0:T(8,128)(2,1)} %bitcast.25), calls=%async_computation.5 | async-start | bytes 2359296 | tf_op jit(solution)/shard_map/all_to_all | solution.py:329
  135.4 2.2 collective-permute-start.2
  137.6 1.3 collective-permute-start.3
  138.9 4.1 %collective-permute-done.3.after = bf16[16,16,128]{2,1,0:T(8,128)(2,1)S(1)} collective-permute-done((bf16[16,16,128]{2,1,0:T(8,128)(2,1)S(1)}, bf16[16,16,128]{2,1,0:T(8,128)(2,1)S(1)}, u32[]{:S(2)}, u32[]{:S(2)}) %collective-permute-start.3) | collective-permute-done | bytes 65568 | tf_op jit(solution)/shard_map/ppermute | solution.py:333
  143.1 1.0 copy-done.3
  144.1 1.0 copy-done.7
  145.2 1.0 copy-done.17
  146.2 1.4 shard_map.83
  149.2 3.3 %all-to-all-done.5.arrived = bf16[288,16,128]{2,1,0:T(8,128)(2,1)} async-done(((bf16[288,16,128]{2,1,0:T(8,128)(2,1)}), bf16[288,16,128]{2,1,0:T(8,128)(2,1)}, u32[]{:S(2)}, u32[]{:S(2)}) %all-to-all-start.5) | async-done | bytes 1179680 | tf_op jit(solution)/shard_map/all_to_all | solution.py:329
  152.6 6.0 %shard_map.84 = (f32[16,16]{1,0:T(8,128)S(1)}, f32[16,16]{1,0:T(8,128)S(1)}, f32[4,16,96]{2,1,0:T(8,128)S(1)}, f32[16,16]{1,0:T(8,128)S(1)}, bf16[288,16,128]{2,1,0:T(8,128)(2,1)S(1)}) custom-call(s32[4,32]{1,0:T(4,128)S(1)} %add_add_fusion.place, bf16[288,16,128]{2,1,0:T(8,128)(2,1)} %all-to-all-done.5.arrived, bf16[4,96,4096]{2,1,0:T(8,128)(2,1)S(1)} %reshape.70.panels, ...), custom_call_target="tpu_custom_call" | custom-call | tf_op jit(solution)/shard_map/pallas_call | solution.py:20
  158.6 17.2 %all_to_all.62.incoming = bf16[288,16,128]{2,1,0:T(8,128)(2,1)S(1)} all-to-all(bf16[288,16,128]{2,1,0:T(8,128)(2,1)S(1)} %get-tuple-element.59), channel_id=1, replica_groups={{0,8,16,24},{1,9,17,25},{2,10,18,26},{3,11,19,27},{4,12,20,28},{5,13,21..., dimensions={0} | all-to-all | bytes 2359296 | tf_op jit(solution)/shard_map/all_to_all | solution.py:305
  176.8 3.4 %all-to-all-start.7 = ((bf16[72,16,128]{2,1,0:T(8,128)(2,1)}), bf16[72,16,128]{2,1,0:T(8,128)(2,1)S(1)}, u32[]{:S(2)}, u32[]{:S(2)}) async-start(bf16[72,16,128]{2,1,0:T(8,128)(2,1)} %copy-done.23), calls=%async_computation.7 | async-start | bytes 589824 | tf_op jit(solution)/shard_map/all_to_all | solution.py:311
  180.2 1.0 copy-done.4
  181.2 1.0 copy-done.8
  182.3 1.0 copy-done.18
  183.3 1.0 copy-done.32
  185.1 1.2 shard_map.87
  187.9 2.0 all-to-all-done.7.incoming
  190.1 20.9 %all_gather.10.groups = bf16[144,16,128]{2,1,0:T(8,128)(2,1)S(1)} all-gather(bf16[9,16,128]{2,1,0:T(8,128)(2,1)S(1)} %shard_map.86), channel_id=1, replica_groups=mesh['src'=16,'mod'=32] {'src'}, dimensions={0}, use_global_device_ids=true | all-gather | bytes 626688 | tf_op jit(solution)/shard_map/all_gather | solution.py:376
  211.0 1.0 copy-done.19
  212.0 3.7 %shard_map.88 = (f32[64,16,128]{2,1,0:T(8,128)S(1)}, f32[16,16]{1,0:T(8,128)S(1)}, bf16[72,16,128]{2,1,0:T(8,128)(2,1)S(1)}, bf16[16,16,128]{2,1,0:T(8,128)(2,1)S(1)}, bf16[16,16,128]{2,1,0:T(8,128)(2,1)S(1)}) custom-call(s32[128]{0:T(128)S(1)} %copy-done.44, s32[8]{0:T(128)S(1)} %copy-done.47, bf16[144,16,128]{2,1,0:T(8,128)(2,1)S(1)} %all_gather.10.groups, ...), custom_call_target="tpu_custom_call" | custom-call | tf_op jit(solution)/shard_map/pallas_call | solution.py:20
  215.7 0.8 copy-done.13
  216.6 16.4 %all_to_all.63 = bf16[72,16,128]{2,1,0:T(8,128)(2,1)S(1)} all-to-all(bf16[72,16,128]{2,1,0:T(8,128)(2,1)S(1)} %get-tuple-element.64), channel_id=1, replica_groups={{0,1,2,3,4,5,6,7},{8,9,10,11,12,13,14,15},{16,17,18,19,20,21,22,23},{24..., dimensions={0} | all-to-all | bytes 589824 | tf_op jit(solution)/shard_map/all_to_all | solution.py:327
  233.0 1.2 broadcast_in_dim.25
  234.2 4.3 %all-to-all-start.9 = ((bf16[288,16,128]{2,1,0:T(8,128)(2,1)}), bf16[288,16,128]{2,1,0:T(8,128)(2,1)}, u32[]{:S(2)}, u32[]{:S(2)}) async-start(bf16[288,16,128]{2,1,0:T(8,128)(2,1)} %bitcast.24), calls=%async_computation.9 | async-start | bytes 2359296 | tf_op jit(solution)/shard_map/all_to_all | solution.py:329
  238.5 1.3 collective-permute-start.4
  239.8 1.3 collective-permute-start.5
  241.1 4.1 %collective-permute-done.5.after = bf16[16,16,128]{2,1,0:T(8,128)(2,1)S(1)} collective-permute-done((bf16[16,16,128]{2,1,0:T(8,128)(2,1)S(1)}, bf16[16,16,128]{2,1,0:T(8,128)(2,1)S(1)}, u32[]{:S(2)}, u32[]{:S(2)}) %collective-permute-start.5) | collective-permute-done | bytes 65568 | tf_op jit(solution)/shard_map/ppermute | solution.py:333
  245.2 1.0 copy-done.11
  246.2 1.0 copy-done.14
  247.3 1.0 copy-done.21
  248.3 1.0 copy-done.26
  249.4 1.4 shard_map.89
  252.4 3.4 %all-to-all-done.9.arrived = bf16[288,16,128]{2,1,0:T(8,128)(2,1)} async-done(((bf16[288,16,128]{2,1,0:T(8,128)(2,1)}), bf16[288,16,128]{2,1,0:T(8,128)(2,1)}, u32[]{:S(2)}, u32[]{:S(2)}) %all-to-all-start.9) | async-done | bytes 1179680 | tf_op jit(solution)/shard_map/all_to_all | solution.py:329
  255.8 6.5 %shard_map.90 = (f32[16,16]{1,0:T(8,128)S(1)}, f32[16,16]{1,0:T(8,128)S(1)}, f32[4,16,96]{2,1,0:T(8,128)}, f32[16,16]{1,0:T(8,128)}, bf16[288,16,128]{2,1,0:T(8,128)(2,1)S(1)}) custom-call(s32[4,32]{1,0:T(4,128)S(1)} %add_add_fusion.place, bf16[288,16,128]{2,1,0:T(8,128)(2,1)} %all-to-all-done.9.arrived, bf16[4,96,4096]{2,1,0:T(8,128)(2,1)S(1)} %reshape.70.panels, ...), custom_call_target="tpu_custom_call" | custom-call | tf_op jit(solution)/shard_map/pallas_call | solution.py:20
  262.3 16.9 %all_to_all.64.incoming = bf16[288,16,128]{2,1,0:T(8,128)(2,1)S(1)} all-to-all(bf16[288,16,128]{2,1,0:T(8,128)(2,1)S(1)} %get-tuple-element.75), channel_id=1, replica_groups={{0,8,16,24},{1,9,17,25},{2,10,18,26},{3,11,19,27},{4,12,20,28},{5,13,21..., dimensions={0} | all-to-all | bytes 2359296 | tf_op jit(solution)/shard_map/all_to_all | solution.py:305
  279.2 1.0 shard_map.91
  280.2 4.4 %all-to-all-start.11 = ((bf16[72,16,128]{2,1,0:T(8,128)(2,1)}), bf16[72,16,128]{2,1,0:T(8,128)(2,1)S(1)}, u32[]{:S(2)}, u32[]{:S(2)}) async-start(bf16[72,16,128]{2,1,0:T(8,128)(2,1)} %shard_map.91), calls=%async_computation.11 | async-start | bytes 589824 | tf_op jit(solution)/shard_map/all_to_all | solution.py:311
  284.7 1.2 shard_map.93
  286.7 7.7 %all-to-all-done.11.incoming = bf16[72,16,128]{2,1,0:T(8,128)(2,1)S(1)} async-done(((bf16[72,16,128]{2,1,0:T(8,128)(2,1)}), bf16[72,16,128]{2,1,0:T(8,128)(2,1)S(1)}, u32[]{:S(2)}, u32[]{:S(2)}) %all-to-all-start.11) | async-done | bytes 294944 | tf_op jit(solution)/shard_map/all_to_all | solution.py:311
  294.6 22.6 %all_gather.11.groups = bf16[144,16,128]{2,1,0:T(8,128)(2,1)S(1)} all-gather(bf16[9,16,128]{2,1,0:T(8,128)(2,1)S(1)} %shard_map.92), channel_id=1, replica_groups=mesh['src'=16,'mod'=32] {'src'}, dimensions={0}, use_global_device_ids=true | all-gather | bytes 626688 | tf_op jit(solution)/shard_map/all_gather | solution.py:376
  317.2 3.9 %shard_map.94 = (f32[64,16,128]{2,1,0:T(8,128)S(1)}, f32[64,16,128]{2,1,0:T(8,128)S(1)}) custom-call(s32[128]{0:T(128)S(1)} %copy-done.45, bf16[144,16,128]{2,1,0:T(8,128)(2,1)S(1)} %all_gather.11.groups, f32[64,16,128]{2,1,0:T(8,128)S(1)} %copy-done.15, f32[64,16,128]{2,1,0:T(8,128)S(1)} %copy-done.34, f32[16,16]{1,0:T(8,128)S(1)} %get-tuple-element.79.norm, ...), custom_call_target="tpu_custom_call" | custom-call | tf_op jit(solution)/shard_map/pallas_call | solution.py:20
  321.1 1.3 copy_bitcast_fusion
  (123 shorter events, 14.6 us)
Async XLA Ops:
  1.6 17.0 %copy-start.52 = (s32[64]{0:T(128)S(1)}, s32[64]{0:T(128)}, u32[]{:S(2)}) copy-start(s32[64]{0:T(128)} %param.11) | copy-start | bytes 772
  2.0 4.2 %copy-start.49 = (s32[64,2]{0,1:T(2,128)}, s32[64,2]{0,1:T(2,128)S(1)}, u32[]{:S(2)}) copy-start(s32[64,2]{0,1:T(2,128)S(1)} %select_reduce_fusion) | copy-start | bytes 1540
  2.3 106.9 %copy-start.46 = (s32[8]{0:T(128)}, s32[8]{0:T(128)S(1)}, u32[]{:S(2)}) copy-start(s32[8]{0:T(128)S(1)} %min.6.own_tile) | copy-start | bytes 100
  5.5 0.8 copy-start
  6.2 17.5 %all-to-all-start = ((bf16[72,16,128]{2,1,0:T(8,128)(2,1)}), bf16[72,16,128]{2,1,0:T(8,128)(2,1)S(1)}, u32[]{:S(2)}, u32[]{:S(2)}) async-start(bf16[72,16,128]{2,1,0:T(8,128)(2,1)} %get-tuple-element.43), calls=%async_computation | async-start | bytes 589824 | tf_op jit(solution)/shard_map/all_to_all | solution.py:327
  13.9 20.8 %collective-permute-start = (bf16[16,16,128]{2,1,0:T(8,128)(2,1)S(1)}, bf16[16,16,128]{2,1,0:T(8,128)(2,1)S(1)}, u32[]{:S(2)}, u32[]{:S(2)}) collective-permute-start(bf16[16,16,128]{2,1,0:T(8,128)(2,1)S(1)} %get-tuple-element.44), channel_id=1, source_target_pairs={{0,1},{1,2},{2,3},{3,4},{4,5},{5,6},{6,7},{7,8},{8,9},{9,10},{10,1... | collective-permute-start | bytes 196616 | tf_op jit(solution)/shard_map/ppermute | solution.py:332
  17.3 17.5 %collective-permute-start.1 = (bf16[16,16,128]{2,1,0:T(8,128)(2,1)S(1)}, bf16[16,16,128]{2,1,0:T(8,128)(2,1)S(1)}, u32[]{:S(2)}, u32[]{:S(2)}) collective-permute-start(bf16[16,16,128]{2,1,0:T(8,128)(2,1)S(1)} %get-tuple-element.45), channel_id=1, source_target_pairs={{1,0},{2,1},{3,2},{4,3},{5,4},{6,5},{7,6},{8,7},{9,8},{10,9},{11,1... | collective-permute-start | bytes 196616 | tf_op jit(solution)/shard_map/ppermute | solution.py:333
  25.0 5.5 %copy-start.51 = (f32[4,96]{1,0:T(4,128)S(1)}, f32[4,96]{1,0:T(4,128)}, u32[]{:S(2)}) copy-start(f32[4,96]{1,0:T(4,128)} %param.9) | copy-start | bytes 4612
  25.0 5.6 %copy-start.48 = (f32[4,16,128]{2,1,0:T(8,128)S(1)}, f32[4,16,128]{2,1,0:T(8,128)}, u32[]{:S(2)}) copy-start(f32[4,16,128]{2,1,0:T(8,128)} %param.7) | copy-start | bytes 98308
  25.0 18.5 %all-to-all-start.1 = ((bf16[288,16,128]{2,1,0:T(8,128)(2,1)}), bf16[288,16,128]{2,1,0:T(8,128)(2,1)}, u32[]{:S(2)}, u32[]{:S(2)}) async-start(bf16[288,16,128]{2,1,0:T(8,128)(2,1)} %bitcast.2), calls=%async_computation.1 | async-start | bytes 2359296 | tf_op jit(solution)/shard_map/all_to_all | solution.py:329
  34.8 1.0 copy-start.1
  36.4 0.8 copy-start.5
  47.8 14.5 %copy-start.39 = (f32[16,16]{1,0:T(8,128)}, f32[16,16]{1,0:T(8,128)S(1)}, u32[]{:S(2)}) copy-start(f32[16,16]{1,0:T(8,128)S(1)} %get-tuple-element.57.refs_2_) | copy-start | bytes 3076
  47.8 61.4 %copy-start.35 = (f32[16,16]{1,0:T(8,128)}, f32[16,16]{1,0:T(8,128)S(1)}, u32[]{:S(2)}) copy-start(f32[16,16]{1,0:T(8,128)S(1)} %get-tuple-element.49.norm.refs_3_) | copy-start | bytes 3076
  62.3 6.5 %copy-start.50 = (s32[64,2]{0,1:T(2,128)S(1)}, s32[64,2]{0,1:T(2,128)}, u32[]{:S(2)}) copy-start(s32[64,2]{0,1:T(2,128)} %copy-done.49) | copy-start | bytes 1540
  62.5 0.7 copy-start.24
  63.2 15.3 %all-to-all-start.3 = ((bf16[72,16,128]{2,1,0:T(8,128)(2,1)}), bf16[72,16,128]{2,1,0:T(8,128)(2,1)S(1)}, u32[]{:S(2)}, u32[]{:S(2)}) async-start(bf16[72,16,128]{2,1,0:T(8,128)(2,1)} %copy-done.24), calls=%async_computation.3 | async-start | bytes 589824 | tf_op jit(solution)/shard_map/all_to_all | solution.py:311
  70.4 43.6 %copy-start.43 = (s32[128]{0:T(128)}, s32[128]{0:T(128)S(1)}, u32[]{:S(2)}) copy-start(s32[128]{0:T(128)S(1)} %reshape.67.slot_tile) | copy-start | bytes 1540
  78.5 30.7 %copy-start.2 = (f32[4,16,16,128]{3,2,1,0:T(8,128)S(1)}, f32[4,16,16,128]{3,2,1,0:T(8,128)}, u32[]{:S(2)}) copy-start(f32[4,16,16,128]{3,2,1,0:T(8,128)} %copy-done) | copy-start | bytes 1572868
  109.2 1.0 copy-start.6
  114.1 0.8 copy-start.16
  131.1 21.5 %all-to-all-start.5 = ((bf16[288,16,128]{2,1,0:T(8,128)(2,1)}), bf16[288,16,128]{2,1,0:T(8,128)(2,1)}, u32[]{:S(2)}, u32[]{:S(2)}) async-start(bf16[288,16,128]{2,1,0:T(8,128)(2,1)} %bitcast.25), calls=%async_computation.5 | async-start | bytes 2359296 | tf_op jit(solution)/shard_map/all_to_all | solution.py:329
  135.4 3.6 %collective-permute-start.2 = (bf16[16,16,128]{2,1,0:T(8,128)(2,1)S(1)}, bf16[16,16,128]{2,1,0:T(8,128)(2,1)S(1)}, u32[]{:S(2)}, u32[]{:S(2)}) collective-permute-start(bf16[16,16,128]{2,1,0:T(8,128)(2,1)S(1)} %get-tuple-element.52), channel_id=1, source_target_pairs={{0,1},{1,2},{2,3},{3,4},{4,5},{5,6},{6,7},{7,8},{8,9},{9,10},{10,1... | collective-permute-start | bytes 196616 | tf_op jit(solution)/shard_map/ppermute | solution.py:332
  137.6 5.4 %collective-permute-start.3 = (bf16[16,16,128]{2,1,0:T(8,128)(2,1)S(1)}, bf16[16,16,128]{2,1,0:T(8,128)(2,1)S(1)}, u32[]{:S(2)}, u32[]{:S(2)}) collective-permute-start(bf16[16,16,128]{2,1,0:T(8,128)(2,1)S(1)} %get-tuple-element.53), channel_id=1, source_target_pairs={{1,0},{2,1},{3,2},{4,3},{5,4},{6,5},{7,6},{8,7},{9,8},{10,9},{11,1... | collective-permute-start | bytes 196616 | tf_op jit(solution)/shard_map/ppermute | solution.py:333
  143.1 1.0 copy-start.3
  144.1 1.0 copy-start.7
  145.2 1.0 copy-start.17
  146.2 6.4 %copy-start.36 = (f32[16,16]{1,0:T(8,128)S(1)}, f32[16,16]{1,0:T(8,128)}, u32[]{:S(2)}) copy-start(f32[16,16]{1,0:T(8,128)} %copy-done.35) | copy-start | bytes 3076
  146.2 6.4 %copy-start.40 = (f32[16,16]{1,0:T(8,128)S(1)}, f32[16,16]{1,0:T(8,128)}, u32[]{:S(2)}) copy-start(f32[16,16]{1,0:T(8,128)} %copy-done.39) | copy-start | bytes 3076
  147.6 0.8 copy-start.25
  148.4 0.8 copy-start.31
  158.6 17.2 %copy-start.37 = (f32[16,16]{1,0:T(8,128)}, f32[16,16]{1,0:T(8,128)S(1)}, u32[]{:S(2)}) copy-start(f32[16,16]{1,0:T(8,128)S(1)} %get-tuple-element.73.refs_2_) | copy-start | bytes 3076
  158.6 17.2 %copy-start.41 = (f32[16,16]{1,0:T(8,128)}, f32[16,16]{1,0:T(8,128)S(1)}, u32[]{:S(2)}) copy-start(f32[16,16]{1,0:T(8,128)S(1)} %get-tuple-element.61.beta) | copy-start | bytes 3076
  176.8 13.2 %all-to-all-start.7 = ((bf16[72,16,128]{2,1,0:T(8,128)(2,1)}), bf16[72,16,128]{2,1,0:T(8,128)(2,1)S(1)}, u32[]{:S(2)}, u32[]{:S(2)}) async-start(bf16[72,16,128]{2,1,0:T(8,128)(2,1)} %copy-done.23), calls=%async_computation.7 | async-start | bytes 589824 | tf_op jit(solution)/shard_map/all_to_all | solution.py:311
  180.2 1.0 copy-start.4
  181.2 1.0 copy-start.8
  182.3 1.0 copy-start.18
  183.3 1.0 copy-start.32
  185.1 25.9 %copy-start.44 = (s32[128]{0:T(128)S(1)}, s32[128]{0:T(128)}, u32[]{:S(2)}) copy-start(s32[128]{0:T(128)} %copy-done.43) | copy-start | bytes 1540
  185.1 25.9 %copy-start.47 = (s32[8]{0:T(128)S(1)}, s32[8]{0:T(128)}, u32[]{:S(2)}) copy-start(s32[8]{0:T(128)} %copy-done.46) | copy-start | bytes 100
  186.3 0.8 copy-start.9
  187.1 0.8 copy-start.20
  189.9 21.0 %copy-start.10 = (f32[64,16,128]{2,1,0:T(8,128)S(1)}, f32[64,16,128]{2,1,0:T(8,128)}, u32[]{:S(2)}) copy-start(f32[64,16,128]{2,1,0:T(8,128)} %copy-done.9) | copy-start | bytes 1572868
  211.0 1.0 copy-start.19
  215.7 0.8 copy-start.13
  234.2 21.6 %all-to-all-start.9 = ((bf16[288,16,128]{2,1,0:T(8,128)(2,1)}), bf16[288,16,128]{2,1,0:T(8,128)(2,1)}, u32[]{:S(2)}, u32[]{:S(2)}) async-start(bf16[288,16,128]{2,1,0:T(8,128)(2,1)} %bitcast.24), calls=%async_computation.9 | async-start | bytes 2359296 | tf_op jit(solution)/shard_map/all_to_all | solution.py:329
  238.5 17.3 %copy-start.38 = (f32[16,16]{1,0:T(8,128)S(1)}, f32[16,16]{1,0:T(8,128)}, u32[]{:S(2)}) copy-start(f32[16,16]{1,0:T(8,128)} %copy-done.37) | copy-start | bytes 3076
  238.5 2.6 collective-permute-start.4
  239.8 5.4 %collective-permute-start.5 = (bf16[16,16,128]{2,1,0:T(8,128)(2,1)S(1)}, bf16[16,16,128]{2,1,0:T(8,128)(2,1)S(1)}, u32[]{:S(2)}, u32[]{:S(2)}) collective-permute-start(bf16[16,16,128]{2,1,0:T(8,128)(2,1)S(1)} %get-tuple-element.67), channel_id=1, source_target_pairs={{1,0},{2,1},{3,2},{4,3},{5,4},{6,5},{7,6},{8,7},{9,8},{10,9},{11,1... | collective-permute-start | bytes 196616 | tf_op jit(solution)/shard_map/ppermute | solution.py:333
  245.2 1.0 copy-start.11
  246.2 1.0 copy-start.14
  247.3 1.0 copy-start.21
  248.3 1.0 copy-start.26
  250.8 0.8 copy-start.27
  251.6 0.8 copy-start.29
  262.3 22.3 %copy-start.30 = (f32[64,16,128]{2,1,0:T(8,128)S(1)}, f32[64,16,128]{2,1,0:T(8,128)}, u32[]{:S(2)}) copy-start(f32[64,16,128]{2,1,0:T(8,128)} %copy-done.29) | copy-start | bytes 1572868
  279.2 5.4 %copy-start.12 = (f32[64,16,128]{2,1,0:T(8,128)S(1)}, f32[64,16,128]{2,1,0:T(8,128)}, u32[]{:S(2)}) copy-start(f32[64,16,128]{2,1,0:T(8,128)} %copy-done.9) | copy-start | bytes 1572868
  279.2 5.4 %copy-start.15 = (f32[64,16,128]{2,1,0:T(8,128)S(1)}, f32[64,16,128]{2,1,0:T(8,128)}, u32[]{:S(2)}) copy-start(f32[64,16,128]{2,1,0:T(8,128)} %copy-done.13) | copy-start | bytes 1572868
  279.2 5.4 %copy-start.22 = (f32[64,16,128]{2,1,0:T(8,128)S(1)}, f32[64,16,128]{2,1,0:T(8,128)}, u32[]{:S(2)}) copy-start(f32[64,16,128]{2,1,0:T(8,128)} %copy-done.20) | copy-start | bytes 1572868
  280.2 14.2 %all-to-all-start.11 = ((bf16[72,16,128]{2,1,0:T(8,128)(2,1)}), bf16[72,16,128]{2,1,0:T(8,128)(2,1)S(1)}, u32[]{:S(2)}, u32[]{:S(2)}) async-start(bf16[72,16,128]{2,1,0:T(8,128)(2,1)} %shard_map.91), calls=%async_computation.11 | async-start | bytes 589824 | tf_op jit(solution)/shard_map/all_to_all | solution.py:311
  284.7 32.5 %copy-start.28 = (f32[64,16,128]{2,1,0:T(8,128)S(1)}, f32[64,16,128]{2,1,0:T(8,128)}, u32[]{:S(2)}) copy-start(f32[64,16,128]{2,1,0:T(8,128)} %copy-done.27) | copy-start | bytes 1572868
  284.7 32.5 %copy-start.45 = (s32[128]{0:T(128)S(1)}, s32[128]{0:T(128)}, u32[]{:S(2)}) copy-start(s32[128]{0:T(128)} %copy-done.43) | copy-start | bytes 1540
  285.9 0.8 copy-start.33
  294.4 22.8 %copy-start.34 = (f32[64,16,128]{2,1,0:T(8,128)S(1)}, f32[64,16,128]{2,1,0:T(8,128)}, u32[]{:S(2)}) copy-start(f32[64,16,128]{2,1,0:T(8,128)} %copy-done.33) | copy-start | bytes 1572868
  (2 other events, 1.4 us)

commit v3 on v2

--- a/solution.py
+++ b/solution.py
@@ -16,7 +16,7 @@
 SMEM = pl.BlockSpec(memory_space=pltpu.SMEM)
 
 
-def call(kernel, outs, args, specs, scratch=(), limit=32 << 20):
+def call(kernel, outs, args, specs, scratch=(), limit=16 << 20):
     return pl.pallas_call(
         kernel,
         out_shape=[jax.ShapeDtypeStruct(shape, dtype) for shape, dtype in outs],
@@ -29,12 +29,25 @@
 
 def solve_small(system, target):
     size = system.shape[0]
-    work = jnp.concatenate([system, target], axis=1)
-    rows = lax.broadcasted_iota(jnp.int32, work.shape, 0)
-    for j in range(size):
-        pivot = work[j : j + 1, :] / work[j : j + 1, j : j + 1]
-        work = jnp.where(rows == j, pivot, work - work[:, j : j + 1] * pivot)
-    return work[:, size:]
+    turned = jnp.concatenate([system, target], axis=0)
+    rows = [jnp.broadcast_to(turned[:, i : i + 1], (2 * size, 128)) for i in range(size)]
+    for p in range(size):
+        base = 8 * ((p + 1) // 8)
+        lead = [rows[i][p - (2 * size - rows[i].shape[0])][None, :] for i in range(size)]
+        keep = base - (2 * size - rows[0].shape[0])
+        pivot = rows[p][keep:] / lead[p]
+        rows = [
+            pivot if i == p else rows[i][keep:] - lead[i] * pivot for i in range(size)
+        ]
+    return rows
+
+
+def matrix_turned(rows):
+    lanes = lax.broadcasted_iota(jnp.int32, rows[0].shape, 1)
+    total = jnp.zeros(rows[0].shape, F32)
+    for i, row in enumerate(rows):
+        total = jnp.where(lanes == i, row, total)
+    return total[:, : len(rows)]
 
 
 def split_three(gram):
@@ -52,10 +65,8 @@
     return total[:, :size] + total[:, size : 2 * size] + total[:, 2 * size : 3 * size]
 
 
-def spread_mixing(mixing):
-    size = mixing.shape[0]
-    turned = mixing.T
-    return [jnp.broadcast_to(turned[:, i : i + 1], (size, 128)) for i in range(size)]
+def read_rows(ref):
+    return [ref[i] for i in range(ref.shape[0])]
 
 
 def mix_tile(tile, spread):
@@ -129,19 +140,19 @@
 
     start = jnp.zeros(groups.shape[1:], F32)
     curvature = join_three(lax.fori_loop(0, src_count, add_group, start))
-    alpha = solve_small(curvature, norm[...])
-    spread = spread_mixing(alpha)
+    spread = solve_small(curvature, norm[...])
     for l in range(tiles):
         fresh[l] = residual[l] - mix_tile(image[l], spread)
-    return alpha, spread
+    return spread
 
 
 def step_kernel(
     src_count, copies, slots, plane, slot_tile, own_tile, groups, residual, smooth, norm,
     fresh, alpha_out, sent, first_plane, last_plane, image,
 ):
-    alpha, _ = advance(src_count, slots, slot_tile, groups, residual, smooth, norm, image, fresh)
-    alpha_out[...] = alpha
+    alpha = advance(src_count, slots, slot_tile, groups, residual, smooth, norm, image, fresh)
+    for i, row in enumerate(alpha):
+        alpha_out[i] = row
     pack(fresh, own_tile, sent, first_plane, last_plane, copies, slots, plane)
 
 
@@ -149,7 +160,7 @@
     src_count, slots, slot_tile, groups, residual, smooth, norm, direction, solution,
     fresh, solution_out, image,
 ):
-    _, spread = advance(src_count, slots, slot_tile, groups, residual, smooth, norm, image, fresh)
+    spread = advance(src_count, slots, slot_tile, groups, residual, smooth, norm, image, fresh)
     for l in range(residual.shape[0]):
         solution_out[l] = solution[l] + mix_tile(direction[l], spread)
 
@@ -174,21 +185,19 @@
         out[l] = diagonal[l : l + 1, :] * tile - beside
 
 
-def regularize_first(plane, field, before, after, diagonal, smooth, gram_own):
+def regularize_first(plane, field, before, after, diagonal, smooth, gram_own, rim_before, rim_after):
+    rim_before[...] = before[...].astype(F32)
+    rim_after[...] = after[...].astype(F32)
     smooth_field(field, before, after, diagonal, smooth, plane)
     gram_own[...] = gram(field, smooth)
 
 
 def regularize_kernel(
-    plane, field, before, after, diagonal, smooth_old, direction, solution, alpha,
-    smooth, gram_own, gram_cross, solution_out,
+    plane, field, before, after, diagonal, smooth_old, gram_own, gram_cross, fresh
 ):
-    smooth_field(field, before, after, diagonal, smooth, plane)
-    gram_own[...] = gram(field, smooth)
     gram_cross[...] = gram(field, smooth_old)
-    spread = spread_mixing(alpha[...])
-    for l in range(field.shape[0]):
-        solution_out[l] = solution[l] + mix_tile(direction[l], spread)
+    smooth_field(field, before, after, diagonal, fresh, plane)
+    gram_own[...] = gram(field, fresh)
 
 
 def data_kernel(first, copies, slots, share, place, arrived, panels, row_weight, *refs):
@@ -209,14 +218,17 @@
     beta = None
     pair = gram_own[...]
     if not first:
-        beta = solve_small(norm_old[...], norm)
-        beta_out[...] = beta
-        cross = small_dot(gram_cross[...], beta, ((1,), (0,)))
-        inner = small_dot(gram_old[...], beta, ((1,), (0,)))
-        pair = pair + cross + cross.T + small_dot(beta, inner, ((0,), (0,)))
+        rows = solve_small(norm_old[...], norm)
+        for i, row in enumerate(rows):
+            beta_out[i] = row
+        beta = matrix_turned(rows)
+        cross = small_dot(beta, gram_cross[...], ((1,), (1,)))
+        inner = small_dot(beta, gram_old[...], ((1,), (0,)))
+        pair = pair + cross + cross.T + small_dot(inner, beta, ((1,), (1,)))
     gram_out[...] = pair
     curvature = share * pair
     empty = jnp.zeros((columns, block_len), BF16)
+    responses, weights = [], []
     for m in range(copies):
         for s in range(slots):
             outgoing[m * per + s] = empty
@@ -224,23 +236,47 @@
         picked = jnp.concatenate([arrived[place[t, f]] for f in range(foot_len)], axis=1)
         response = nt(picked, panels[t])
         if not first:
-            response = response + small_dot(beta, response_old[t], ((0,), (0,)))
+            response = response + small_dot(beta, response_old[t], ((1,), (0,)))
         response_out[t] = response
         weighted = response * row_weight[t : t + 1, :]
-        curvature = curvature + gram_halves(halves(response), halves(weighted))
-        shares = jnp.dot(weighted.astype(BF16), panels[t], preferred_element_type=F32).astype(BF16)
+        responses.append(response)
+        weights.append(weighted)
+    for t in range(tx_here):
+        shares = jnp.dot(
+            weights[t].astype(BF16), panels[t], preferred_element_type=F32
+        ).astype(BF16)
         for f in range(foot_len):
             outgoing[place[t, f]] = shares[:, f * block_len : (f + 1) * block_len]
+    curvature = curvature + gram_halves(
+        halves(jnp.concatenate(responses, axis=1)), halves(jnp.concatenate(weights, axis=1))
+    )
     pieces = split_three(curvature)
     for m in range(copies):
         outgoing[m * per + slots] = pieces
 
 
-def mix_kernel(fresh, smooth_fresh, direction, smooth, beta, direction_out, smooth_out):
-    spread = spread_mixing(beta[...])
+def mix_kernel(
+    plane, fresh, before, after, diagonal, direction, rim_before, rim_after, beta,
+    direction_out, smooth_out, rim_before_out, rim_after_out,
+):
+    spread = read_rows(beta)
     for l in range(fresh.shape[0]):
         direction_out[l] = fresh[l] + mix_tile(direction[l], spread)
-        smooth_out[l] = smooth_fresh[l] + mix_tile(smooth[l], spread)
+    for y in range(plane):
+        rim_before_out[y] = before[y].astype(F32) + mix_tile(rim_before[y], spread)
+        rim_after_out[y] = after[y].astype(F32) + mix_tile(rim_after[y], spread)
+    smooth_field(direction_out, rim_before_out, rim_after_out, diagonal, smooth_out, plane)
+
+
+def gather_kernel(*refs):
+    count = (len(refs) - 1) // 2
+    directions, alphas, out = refs[:count], refs[count : 2 * count], refs[-1]
+    spreads = [read_rows(alpha) for alpha in alphas]
+    for l in range(out.shape[0]):
+        total = mix_tile(directions[0][l], spreads[0])
+        for direction, spread in zip(directions[1:], spreads[1:]):
+            total = total + mix_tile(direction[l], spread)
+        out[l] = total
 
 
 def sum_kernel(copies, blocks, slots, incoming, handed):
@@ -298,6 +334,8 @@
     field = ((tiles, columns, block_len), F32)
     small = ((columns, columns), F32)
     edge = ((plane, columns, block_len), BF16)
+    factors = ((columns, columns, 128), F32)
+    rim = ((plane, columns, block_len), F32)
     packet = ((copies * per, columns, block_len), BF16)
     part = ((inner * per, columns, block_len), BF16)
 
@@ -320,21 +358,20 @@
         (own_tile, residual),
         (SMEM, VMEM),
     )
-    solution = jnp.zeros_like(residual)
-    direction = smooth = norm = response = gram_pair = alpha = None
+    direction = smooth = norm = response = gram_pair = rim_before = rim_after = None
+    directions, alphas = [], []
     for iteration in range(ITERS):
-        first = iteration == 0
         across = lax.all_to_all(sent, "mod", 0, 0, tiled=True, axis_index_groups=along_y)
+        before = lax.ppermute(last_plane, "mod", up)
+        after = lax.ppermute(first_plane, "mod", down)
         across = jnp.broadcast_to(across[None], (across_x,) + across.shape)
         arrived = lax.all_to_all(
             across.reshape(packet[0]), "mod", 0, 0, tiled=True, axis_index_groups=along_x
         )
-        before = lax.ppermute(last_plane, "mod", up)
-        after = lax.ppermute(first_plane, "mod", down)
-        if first:
-            smooth, gram_own = call(
+        if iteration == 0:
+            smooth, gram_own, rim_before, rim_after = call(
                 functools.partial(regularize_first, plane),
-                [field, small],
+                [field, small, rim, rim],
                 (residual, before, after, diagonal),
                 (VMEM,) * 4,
             )
@@ -347,25 +384,37 @@
             )
             incoming = reduced(outgoing)
         else:
-            smooth_fresh, gram_own, gram_cross, solution = call(
+            gram_own, gram_cross = call(
                 functools.partial(regularize_kernel, plane),
-                [field, small, small, field],
-                (residual, before, after, diagonal, smooth, direction, solution, alpha),
-                (VMEM,) * 8,
+                [small, small],
+                (residual, before, after, diagonal, smooth),
+                (VMEM,) * 5,
+                scratch=(pltpu.VMEM(field[0], F32),),
             )
             norm, beta, response, gram_pair, outgoing = call(
                 functools.partial(data_kernel, False, copies, slots, share),
-                [small, small, responses, small, packet],
-                (place, arrived, flat_panels, row_weight, gram_own, gram_cross, gram_pair, norm,
-                 response),
+                [small, factors, responses, small, packet],
+                (place, arrived, flat_panels, row_weight, gram_own, gram_cross,
+                 gram_pair, norm, response),
                 (SMEM,) + (VMEM,) * 8,
             )
             incoming = reduced(outgoing)
-            direction, smooth = call(
-                mix_kernel,
-                [field, field],
-                (residual, smooth_fresh, direction, smooth, beta),
-                (VMEM,) * 5,
+            direction, smooth, rim_before, rim_after = call(
+                functools.partial(mix_kernel, plane),
+                [field, field, rim, rim],
+                (residual, before, after, diagonal,
+                 direction, rim_before,
+                 rim_after, beta),
+                (VMEM,) * 8,
+            )
+        directions.append(direction)
+        if iteration + 1 == ITERS:
+            (solution,) = call(
+                gather_kernel,
+                [field],
+                (*directions[:-1],
+                 *alphas),
+                (VMEM,) * (2 * len(alphas)),
             )
         (handed,) = call(
             functools.partial(sum_kernel, inner, 1, slots),
@@ -377,16 +426,18 @@
         if iteration + 1 < ITERS:
             residual, alpha, sent, first_plane, last_plane = call(
                 functools.partial(step_kernel, src_count, inner, slots, plane),
-                [field, small, part, edge, edge],
+                [field, factors, part, edge, edge],
                 (slot_tile, own_tile, groups, residual, smooth, norm),
                 (SMEM, SMEM) + (VMEM,) * 4,
                 scratch=(image,),
             )
+            alphas.append(alpha)
         else:
             residual, solution = call(
                 functools.partial(last_kernel, src_count, slots),
                 [field, field],
-                (slot_tile, groups, residual, smooth, norm, direction, solution),
+                (slot_tile, groups, residual, smooth, norm, direction,
+                 solution),
                 (SMEM,) + (VMEM,) * 6,
                 scratch=(image,),
             )

time: 325 us -> 314 us (0.966)
  Pallas kernels: 37.7 us -> 27.2 us
  waiting for transfers between devices: 44.1 us -> 48.4 us
    pallas_call x18 -> x19, Pallas kernels: 37.7 us -> 27.2 us  [call(): pl.pallas_call(kernel, out_shape=[jax.ShapeDtypeStruct(shape, dtype) for...]
    all_to_all x3, waiting for transfers between devices: 13.1 us -> 18.7 us  [shards(): lax.all_to_all(across.reshape(packet[0]), 'mod', 0, 0, tiled=True, axis_i...]
    unnamed x108 -> x118, local copies, waits for them, and re-layouts: 26.5 us -> 24.7 us
where the time goes in v3:
time: 314 us; the launch traced here: 312 us
  blocking collectives  153 us (49%)
  waiting for transfers between devices  48.4 us (15%)
  starting transfers between devices  45.2 us (14%)
  local copies, waits for them, and re-layouts  35.8 us (11%)
  Pallas kernels  27.2 us (9%)
    all_gather x3, blocking collectives, shards(): groups = lax.all_gather(handed, 'src', axis=0, tiled=True)  71 us
    all_to_all x3, blocking collectives, reduced(): lax.all_to_all(outgoing, 'mod', 0, 0, tiled=True, axis_index_groups=along_x)  49 us
    all_to_all x2, blocking collectives, shards(): lax.all_to_all(sent, 'mod', 0, 0, tiled=True, axis_index_groups=along_y)  33.3 us
    pallas_call x19, Pallas kernels, call(): pl.pallas_call(kernel, out_shape=[jax.ShapeDtypeStruct(shape, dtype) for...  27.2 us
    unnamed x118, local copies, waits for them, and re-layouts  24.7 us
    all_to_all x3, waiting for transfers between devices, shards(): lax.all_to_all(across.reshape(packet[0]), 'mod', 0, 0, tiled=True, axis_i...  18.7 us
    all_to_all x3, waiting for transfers between devices, reduced(): lax.all_to_all(halfway, 'mod', 0, 0, tiled=True, axis_index_groups=along_y)  16.6 us
    all_to_all x3, starting transfers between devices, shards(): lax.all_to_all(across.reshape(packet[0]), 'mod', 0, 0, tiled=True, axis_i...  14.3 us
  transfers between devices with their start and end apart: 13, of which 9 were waited for; matrix products, arithmetic and copies ran while one was open for 2% of the time, Pallas kernels for 2%

profile of v3, /device:TPU:1, one launch (start us, length us, event | category | flops | bytes accessed | tf_op | source)
XLA Modules:
  0.0 311.6 jit_solution(10868329863412507963)
XLA Ops:
  0.7 0.8 copy.47
  2.3 1.4 copy.61
  3.7 1.8 shard_map.77
  6.2 7.7 %all-to-all-start = ((bf16[72,16,128]{2,1,0:T(8,128)(2,1)}), bf16[72,16,128]{2,1,0:T(8,128)(2,1)S(1)}, u32[]{:S(2)}, u32[]{:S(2)}) async-start(bf16[72,16,128]{2,1,0:T(8,128)(2,1)} %get-tuple-element.43), calls=%async_computation | async-start | bytes 589824 | tf_op jit(solution)/shard_map/all_to_all | solution.py:364
  13.9 3.4 %collective-permute-start = (bf16[16,16,128]{2,1,0:T(8,128)(2,1)S(1)}, bf16[16,16,128]{2,1,0:T(8,128)(2,1)S(1)}, u32[]{:S(2)}, u32[]{:S(2)}) collective-permute-start(bf16[16,16,128]{2,1,0:T(8,128)(2,1)S(1)} %get-tuple-element.44), channel_id=1, source_target_pairs={{0,1},{1,2},{2,3},{3,4},{4,5},{5,6},{6,7},{7,8},{8,9},{9,10},{10,1... | collective-permute-start | bytes 196616 | tf_op jit(solution)/shard_map/ppermute | solution.py:365
  17.2 1.3 collective-permute-start.1
  18.8 5.0 %all-to-all-done = bf16[72,16,128]{2,1,0:T(8,128)(2,1)S(1)} async-done(((bf16[72,16,128]{2,1,0:T(8,128)(2,1)}), bf16[72,16,128]{2,1,0:T(8,128)(2,1)S(1)}, u32[]{:S(2)}, u32[]{:S(2)}) %all-to-all-start) | async-done | bytes 294944 | tf_op jit(solution)/shard_map/all_to_all | solution.py:364
  23.8 1.2 broadcast_in_dim.20
  25.0 5.5 %all-to-all-start.1 = ((bf16[288,16,128]{2,1,0:T(8,128)(2,1)}), bf16[288,16,128]{2,1,0:T(8,128)(2,1)}, u32[]{:S(2)}, u32[]{:S(2)}) async-start(bf16[288,16,128]{2,1,0:T(8,128)(2,1)} %bitcast.2), calls=%async_computation.1 | async-start | bytes 2359296 | tf_op jit(solution)/shard_map/all_to_all | solution.py:368
  30.6 4.1 %reshape.70.panels = bf16[4,96,4096]{2,1,0:T(8,128)(2,1)S(1)} reshape(bf16[4,96,32,128]{3,2,1,0:T(8,128)(2,1)} %param.8) | data formatting | bytes 6291456 | tf_op jit(solution)/shard_map/reshape | solution.py:326
  34.8 1.0 copy-done.1
  36.3 0.8 copy-done.14
  38.5 5.0 %all-to-all-done.1.arrived = bf16[288,16,128]{2,1,0:T(8,128)(2,1)} async-done(((bf16[288,16,128]{2,1,0:T(8,128)(2,1)}), bf16[288,16,128]{2,1,0:T(8,128)(2,1)}, u32[]{:S(2)}, u32[]{:S(2)}) %all-to-all-start.1) | async-done | bytes 1179680 | tf_op jit(solution)/shard_map/all_to_all | solution.py:368
  43.5 2.7 shard_map.79
  46.3 14.5 %all_to_all.60.incoming = bf16[288,16,128]{2,1,0:T(8,128)(2,1)S(1)} all-to-all(bf16[288,16,128]{2,1,0:T(8,128)(2,1)S(1)} %get-tuple-element.47), channel_id=1, replica_groups={{0,8,16,24},{1,9,17,25},{2,10,18,26},{3,11,19,27},{4,12,20,28},{5,13,21..., dimensions={0} | all-to-all | bytes 2359296 | tf_op jit(solution)/shard_map/all_to_all | solution.py:343
  61.7 5.5 %all-to-all-start.3 = ((bf16[72,16,128]{2,1,0:T(8,128)(2,1)}), bf16[72,16,128]{2,1,0:T(8,128)(2,1)S(1)}, u32[]{:S(2)}, u32[]{:S(2)}) async-start(bf16[72,16,128]{2,1,0:T(8,128)(2,1)} %copy-done.21), calls=%async_computation.3 | async-start | bytes 589824 | tf_op jit(solution)/shard_map/all_to_all | solution.py:349
  67.5 9.5 %all-to-all-done.3.incoming = bf16[72,16,128]{2,1,0:T(8,128)(2,1)S(1)} async-done(((bf16[72,16,128]{2,1,0:T(8,128)(2,1)}), bf16[72,16,128]{2,1,0:T(8,128)(2,1)S(1)}, u32[]{:S(2)}, u32[]{:S(2)}) %all-to-all-start.3) | async-done | bytes 294944 | tf_op jit(solution)/shard_map/all_to_all | solution.py:349
  77.1 30.5 %all_gather.9.groups = bf16[144,16,128]{2,1,0:T(8,128)(2,1)S(1)} all-gather(bf16[9,16,128]{2,1,0:T(8,128)(2,1)S(1)} %shard_map.81), channel_id=1, replica_groups=mesh['src'=16,'mod'=32] {'src'}, dimensions={0}, use_global_device_ids=true | all-gather | bytes 626688 | tf_op jit(solution)/shard_map/all_gather | solution.py:425
  107.6 1.0 copy-done.15
  108.7 2.4 shard_map.82
  111.9 15.1 %all_to_all.61 = bf16[72,16,128]{2,1,0:T(8,128)(2,1)S(1)} all-to-all(bf16[72,16,128]{2,1,0:T(8,128)(2,1)S(1)} %get-tuple-element.50), channel_id=1, replica_groups={{0,1,2,3,4,5,6,7},{8,9,10,11,12,13,14,15},{16,17,18,19,20,21,22,23},{24..., dimensions={0} | all-to-all | bytes 589824 | tf_op jit(solution)/shard_map/all_to_all | solution.py:364
  126.9 1.2 broadcast_in_dim.21
  128.1 4.4 %all-to-all-start.5 = ((bf16[288,16,128]{2,1,0:T(8,128)(2,1)}), bf16[288,16,128]{2,1,0:T(8,128)(2,1)}, u32[]{:S(2)}, u32[]{:S(2)}) async-start(bf16[288,16,128]{2,1,0:T(8,128)(2,1)} %bitcast.26), calls=%async_computation.5 | async-start | bytes 2359296 | tf_op jit(solution)/shard_map/all_to_all | solution.py:368
  132.5 2.2 collective-permute-start.2
  134.8 1.3 collective-permute-start.3
  136.1 4.1 %collective-permute-done.3.after = bf16[16,16,128]{2,1,0:T(8,128)(2,1)S(1)} collective-permute-done((bf16[16,16,128]{2,1,0:T(8,128)(2,1)S(1)}, bf16[16,16,128]{2,1,0:T(8,128)(2,1)S(1)}, u32[]{:S(2)}, u32[]{:S(2)}) %collective-permute-start.3) | collective-permute-done | bytes 65568 | tf_op jit(solution)/shard_map/ppermute | solution.py:366
  140.2 1.0 copy-done.9
  141.2 1.0 copy-done.16
  142.3 0.8 shard_map.83
  143.8 5.9 %all-to-all-done.5.arrived = bf16[288,16,128]{2,1,0:T(8,128)(2,1)} async-done(((bf16[288,16,128]{2,1,0:T(8,128)(2,1)}), bf16[288,16,128]{2,1,0:T(8,128)(2,1)}, u32[]{:S(2)}, u32[]{:S(2)}) %all-to-all-start.5) | async-done | bytes 1179680 | tf_op jit(solution)/shard_map/all_to_all | solution.py:368
  149.7 3.4 %shard_map.84 = (f32[16,16]{1,0:T(8,128)S(1)}, f32[16,16,128]{2,1,0:T(8,128)S(1)}, f32[4,16,96]{2,1,0:T(8,128)S(1)}, f32[16,16]{1,0:T(8,128)S(1)}, bf16[288,16,128]{2,1,0:T(8,128)(2,1)S(1)}) custom-call(s32[4,32]{1,0:T(4,128)S(1)} %add_add_fusion.place, bf16[288,16,128]{2,1,0:T(8,128)(2,1)} %all-to-all-done.5.arrived, ...), custom_call_target="tpu_custom_call" | custom-call | tf_op jit(solution)/shard_map/pallas_call | solution.py:20
  153.2 17.2 %all_to_all.62.incoming = bf16[288,16,128]{2,1,0:T(8,128)(2,1)S(1)} all-to-all(bf16[288,16,128]{2,1,0:T(8,128)(2,1)S(1)} %get-tuple-element.58), channel_id=1, replica_groups={{0,8,16,24},{1,9,17,25},{2,10,18,26},{3,11,19,27},{4,12,20,28},{5,13,21..., dimensions={0} | all-to-all | bytes 2359296 | tf_op jit(solution)/shard_map/all_to_all | solution.py:343
  171.4 3.4 %all-to-all-start.7 = ((bf16[72,16,128]{2,1,0:T(8,128)(2,1)}), bf16[72,16,128]{2,1,0:T(8,128)(2,1)S(1)}, u32[]{:S(2)}, u32[]{:S(2)}) async-start(bf16[72,16,128]{2,1,0:T(8,128)(2,1)} %copy-done.20), calls=%async_computation.7 | async-start | bytes 589824 | tf_op jit(solution)/shard_map/all_to_all | solution.py:349
  174.8 1.0 copy-done.3
  175.9 1.0 copy-done.10
  176.9 0.8 copy-done.23
  177.8 0.9 copy-done.29
  178.7 0.9 copy-done.31
  179.6 0.9 copy-done.39
  180.5 1.0 shard_map.87
  184.7 19.5 %all_gather.10.groups = bf16[144,16,128]{2,1,0:T(8,128)(2,1)S(1)} all-gather(bf16[9,16,128]{2,1,0:T(8,128)(2,1)S(1)} %shard_map.86), channel_id=1, replica_groups=mesh['src'=16,'mod'=32] {'src'}, dimensions={0}, use_global_device_ids=true | all-gather | bytes 626688 | tf_op jit(solution)/shard_map/all_gather | solution.py:425
  204.2 1.0 copy-done.18
  206.5 2.4 shard_map.88
  208.9 0.8 copy-done.5
  209.7 18.2 %all_to_all.63 = bf16[72,16,128]{2,1,0:T(8,128)(2,1)S(1)} all-to-all(bf16[72,16,128]{2,1,0:T(8,128)(2,1)S(1)} %get-tuple-element.64), channel_id=1, replica_groups={{0,1,2,3,4,5,6,7},{8,9,10,11,12,13,14,15},{16,17,18,19,20,21,22,23},{24..., dimensions={0} | all-to-all | bytes 589824 | tf_op jit(solution)/shard_map/all_to_all | solution.py:364
  227.9 1.2 broadcast_in_dim.22
  229.1 4.4 %all-to-all-start.9 = ((bf16[288,16,128]{2,1,0:T(8,128)(2,1)}), bf16[288,16,128]{2,1,0:T(8,128)(2,1)}, u32[]{:S(2)}, u32[]{:S(2)}) async-start(bf16[288,16,128]{2,1,0:T(8,128)(2,1)} %bitcast.27), calls=%async_computation.9 | async-start | bytes 2359296 | tf_op jit(solution)/shard_map/all_to_all | solution.py:368
  233.5 1.3 collective-permute-start.4
  234.8 1.3 collective-permute-start.5
  236.1 4.1 %collective-permute-done.5.after = bf16[16,16,128]{2,1,0:T(8,128)(2,1)S(1)} collective-permute-done((bf16[16,16,128]{2,1,0:T(8,128)(2,1)S(1)}, bf16[16,16,128]{2,1,0:T(8,128)(2,1)S(1)}, u32[]{:S(2)}, u32[]{:S(2)}) %collective-permute-start.5) | collective-permute-done | bytes 65568 | tf_op jit(solution)/shard_map/ppermute | solution.py:366
  240.2 1.0 copy-done.6
  241.3 1.0 copy-done.19
  242.3 0.8 shard_map.89
  243.2 7.7 %all-to-all-done.9.arrived = bf16[288,16,128]{2,1,0:T(8,128)(2,1)} async-done(((bf16[288,16,128]{2,1,0:T(8,128)(2,1)}), bf16[288,16,128]{2,1,0:T(8,128)(2,1)}, u32[]{:S(2)}, u32[]{:S(2)}) %all-to-all-start.9) | async-done | bytes 1179680 | tf_op jit(solution)/shard_map/all_to_all | solution.py:368
  250.9 3.9 %shard_map.90 = (f32[16,16]{1,0:T(8,128)S(1)}, f32[16,16,128]{2,1,0:T(8,128)S(1)}, f32[4,16,96]{2,1,0:T(8,128)}, f32[16,16]{1,0:T(8,128)}, bf16[288,16,128]{2,1,0:T(8,128)(2,1)S(1)}) custom-call(s32[4,32]{1,0:T(4,128)S(1)} %add_add_fusion.place, bf16[288,16,128]{2,1,0:T(8,128)(2,1)} %all-to-all-done.9.arrived, bf16[4,96,4096]{2,1,0:T(8,128)(2,1)S(1)} %reshape.70.panels, ...), custom_call_target="tpu_custom_call" | custom-call | tf_op jit(solution)/shard_map/pallas_call | solution.py:20
  254.8 17.4 %all_to_all.64.incoming = bf16[288,16,128]{2,1,0:T(8,128)(2,1)S(1)} all-to-all(bf16[288,16,128]{2,1,0:T(8,128)(2,1)S(1)} %get-tuple-element.72), channel_id=1, replica_groups={{0,8,16,24},{1,9,17,25},{2,10,18,26},{3,11,19,27},{4,12,20,28},{5,13,21..., dimensions={0} | all-to-all | bytes 2359296 | tf_op jit(solution)/shard_map/all_to_all | solution.py:343
  272.2 1.0 shard_map.91
  273.1 3.6 %all-to-all-start.11 = ((bf16[72,16,128]{2,1,0:T(8,128)(2,1)}), bf16[72,16,128]{2,1,0:T(8,128)(2,1)S(1)}, u32[]{:S(2)}, u32[]{:S(2)}) async-start(bf16[72,16,128]{2,1,0:T(8,128)(2,1)} %shard_map.91), calls=%async_computation.11 | async-start | bytes 589824 | tf_op jit(solution)/shard_map/all_to_all | solution.py:349
  276.8 1.1 shard_map.94.solution
  278.0 1.7 shard_map.93
  279.6 6.9 %all-to-all-done.11.incoming = bf16[72,16,128]{2,1,0:T(8,128)(2,1)S(1)} async-done(((bf16[72,16,128]{2,1,0:T(8,128)(2,1)}), bf16[72,16,128]{2,1,0:T(8,128)(2,1)S(1)}, u32[]{:S(2)}, u32[]{:S(2)}) %all-to-all-start.11) | async-done | bytes 294944 | tf_op jit(solution)/shard_map/all_to_all | solution.py:349
  286.7 21.0 %all_gather.11.groups = bf16[144,16,128]{2,1,0:T(8,128)(2,1)S(1)} all-gather(bf16[9,16,128]{2,1,0:T(8,128)(2,1)S(1)} %shard_map.92), channel_id=1, replica_groups=mesh['src'=16,'mod'=32] {'src'}, dimensions={0}, use_global_device_ids=true | all-gather | bytes 626688 | tf_op jit(solution)/shard_map/all_gather | solution.py:425
  307.7 2.7 shard_map.95
  310.3 1.3 copy_bitcast_fusion
  (133 shorter events, 12.4 us)
Async XLA Ops:
  1.6 16.9 %copy-start.57 = (s32[64]{0:T(128)S(1)}, s32[64]{0:T(128)}, u32[]{:S(2)}) copy-start(s32[64]{0:T(128)} %param.11) | copy-start | bytes 772
  2.3 105.3 %copy-start.53 = (s32[8]{0:T(128)}, s32[8]{0:T(128)S(1)}, u32[]{:S(2)}) copy-start(s32[8]{0:T(128)S(1)} %min.6.own_tile) | copy-start | bytes 100
  5.4 0.8 copy-start
  6.2 17.5 %all-to-all-start = ((bf16[72,16,128]{2,1,0:T(8,128)(2,1)}), bf16[72,16,128]{2,1,0:T(8,128)(2,1)S(1)}, u32[]{:S(2)}, u32[]{:S(2)}) async-start(bf16[72,16,128]{2,1,0:T(8,128)(2,1)} %get-tuple-element.43), calls=%async_computation | async-start | bytes 589824 | tf_op jit(solution)/shard_map/all_to_all | solution.py:364
  13.9 20.8 %collective-permute-start = (bf16[16,16,128]{2,1,0:T(8,128)(2,1)S(1)}, bf16[16,16,128]{2,1,0:T(8,128)(2,1)S(1)}, u32[]{:S(2)}, u32[]{:S(2)}) collective-permute-start(bf16[16,16,128]{2,1,0:T(8,128)(2,1)S(1)} %get-tuple-element.44), channel_id=1, source_target_pairs={{0,1},{1,2},{2,3},{3,4},{4,5},{5,6},{6,7},{7,8},{8,9},{9,10},{10,1... | collective-permute-start | bytes 196616 | tf_op jit(solution)/shard_map/ppermute | solution.py:365
  17.2 17.5 %collective-permute-start.1 = (bf16[16,16,128]{2,1,0:T(8,128)(2,1)S(1)}, bf16[16,16,128]{2,1,0:T(8,128)(2,1)S(1)}, u32[]{:S(2)}, u32[]{:S(2)}) collective-permute-start(bf16[16,16,128]{2,1,0:T(8,128)(2,1)S(1)} %get-tuple-element.45), channel_id=1, source_target_pairs={{1,0},{2,1},{3,2},{4,3},{5,4},{6,5},{7,6},{8,7},{9,8},{10,9},{11,1... | collective-permute-start | bytes 196616 | tf_op jit(solution)/shard_map/ppermute | solution.py:366
  24.9 5.5 %copy-start.56 = (f32[4,96]{1,0:T(4,128)S(1)}, f32[4,96]{1,0:T(4,128)}, u32[]{:S(2)}) copy-start(f32[4,96]{1,0:T(4,128)} %param.9) | copy-start | bytes 4612
  25.0 5.6 %copy-start.55 = (f32[4,16,128]{2,1,0:T(8,128)S(1)}, f32[4,16,128]{2,1,0:T(8,128)}, u32[]{:S(2)}) copy-start(f32[4,16,128]{2,1,0:T(8,128)} %param.7) | copy-start | bytes 98308
  25.0 18.5 %all-to-all-start.1 = ((bf16[288,16,128]{2,1,0:T(8,128)(2,1)}), bf16[288,16,128]{2,1,0:T(8,128)(2,1)}, u32[]{:S(2)}, u32[]{:S(2)}) async-start(bf16[288,16,128]{2,1,0:T(8,128)(2,1)} %bitcast.2), calls=%async_computation.1 | async-start | bytes 2359296 | tf_op jit(solution)/shard_map/all_to_all | solution.py:368
  34.7 1.0 copy-start.1
  36.3 0.8 copy-start.14
  46.2 14.5 %copy-start.42 = (f32[4,16,96]{2,1,0:T(8,128)}, f32[4,16,96]{2,1,0:T(8,128)S(1)}, u32[]{:S(2)}) copy-start(f32[4,16,96]{2,1,0:T(8,128)S(1)} %get-tuple-element.57.refs_4_) | copy-start | bytes 73732
  46.2 14.5 %copy-start.48 = (f32[16,16]{1,0:T(8,128)}, f32[16,16]{1,0:T(8,128)S(1)}, u32[]{:S(2)}) copy-start(f32[16,16]{1,0:T(8,128)S(1)} %get-tuple-element.56.refs_2_) | copy-start | bytes 3076
  46.2 61.4 %copy-start.44 = (f32[16,16]{1,0:T(8,128)}, f32[16,16]{1,0:T(8,128)S(1)}, u32[]{:S(2)}) copy-start(f32[16,16]{1,0:T(8,128)S(1)} %get-tuple-element.49.norm.refs_3_) | copy-start | bytes 3076
  61.0 0.7 copy-start.21
  61.7 15.2 %all-to-all-start.3 = ((bf16[72,16,128]{2,1,0:T(8,128)(2,1)}), bf16[72,16,128]{2,1,0:T(8,128)(2,1)S(1)}, u32[]{:S(2)}, u32[]{:S(2)}) async-start(bf16[72,16,128]{2,1,0:T(8,128)(2,1)} %copy-done.21), calls=%async_computation.3 | async-start | bytes 589824 | tf_op jit(solution)/shard_map/all_to_all | solution.py:349
  67.5 43.6 %copy-start.50 = (s32[128]{0:T(128)}, s32[128]{0:T(128)S(1)}, u32[]{:S(2)}) copy-start(s32[128]{0:T(128)S(1)} %reshape.67.slot_tile) | copy-start | bytes 1540
  76.9 30.7 %copy-start.2 = (f32[4,16,16,128]{3,2,1,0:T(8,128)S(1)}, f32[4,16,16,128]{3,2,1,0:T(8,128)}, u32[]{:S(2)}) copy-start(f32[4,16,16,128]{3,2,1,0:T(8,128)} %copy-done) | copy-start | bytes 1572868
  107.6 1.0 copy-start.15
  111.1 0.8 copy-start.8
  111.9 15.1 %copy-start.24 = (f32[16,16,128]{2,1,0:T(8,128)}, f32[16,16,128]{2,1,0:T(8,128)S(1)}, u32[]{:S(2)}) copy-start(f32[16,16,128]{2,1,0:T(8,128)S(1)} %get-tuple-element.80.refs_2_) | copy-start | bytes 393220
  128.1 21.6 %copy-start.43 = (f32[4,16,96]{2,1,0:T(8,128)S(1)}, f32[4,16,96]{2,1,0:T(8,128)}, u32[]{:S(2)}) copy-start(f32[4,16,96]{2,1,0:T(8,128)} %copy-done.42) | copy-start | bytes 73732
  128.1 21.6 %copy-start.45 = (f32[16,16]{1,0:T(8,128)S(1)}, f32[16,16]{1,0:T(8,128)}, u32[]{:S(2)}) copy-start(f32[16,16]{1,0:T(8,128)} %copy-done.44) | copy-start | bytes 3076
  128.1 21.6 %copy-start.49 = (f32[16,16]{1,0:T(8,128)S(1)}, f32[16,16]{1,0:T(8,128)}, u32[]{:S(2)}) copy-start(f32[16,16]{1,0:T(8,128)} %copy-done.48) | copy-start | bytes 3076
  128.1 21.6 %all-to-all-start.5 = ((bf16[288,16,128]{2,1,0:T(8,128)(2,1)}), bf16[288,16,128]{2,1,0:T(8,128)(2,1)}, u32[]{:S(2)}, u32[]{:S(2)}) async-start(bf16[288,16,128]{2,1,0:T(8,128)(2,1)} %bitcast.26), calls=%async_computation.5 | async-start | bytes 2359296 | tf_op jit(solution)/shard_map/all_to_all | solution.py:368
  132.5 3.6 %collective-permute-start.2 = (bf16[16,16,128]{2,1,0:T(8,128)(2,1)S(1)}, bf16[16,16,128]{2,1,0:T(8,128)(2,1)S(1)}, u32[]{:S(2)}, u32[]{:S(2)}) collective-permute-start(bf16[16,16,128]{2,1,0:T(8,128)(2,1)S(1)} %get-tuple-element.52), channel_id=1, source_target_pairs={{0,1},{1,2},{2,3},{3,4},{4,5},{5,6},{6,7},{7,8},{8,9},{9,10},{10,1... | collective-permute-start | bytes 196616 | tf_op jit(solution)/shard_map/ppermute | solution.py:365
  134.8 5.4 %collective-permute-start.3 = (bf16[16,16,128]{2,1,0:T(8,128)(2,1)S(1)}, bf16[16,16,128]{2,1,0:T(8,128)(2,1)S(1)}, u32[]{:S(2)}, u32[]{:S(2)}) collective-permute-start(bf16[16,16,128]{2,1,0:T(8,128)(2,1)S(1)} %get-tuple-element.53), channel_id=1, source_target_pairs={{1,0},{2,1},{3,2},{4,3},{5,4},{6,5},{7,6},{8,7},{9,8},{10,9},{11,1... | collective-permute-start | bytes 196616 | tf_op jit(solution)/shard_map/ppermute | solution.py:366
  140.2 1.0 copy-start.9
  141.2 1.0 copy-start.16
  153.2 17.3 %copy-start.38 = (f32[16,16,128]{2,1,0:T(8,128)}, f32[16,16,128]{2,1,0:T(8,128)S(1)}, u32[]{:S(2)}) copy-start(f32[16,16,128]{2,1,0:T(8,128)S(1)} %get-tuple-element.61.beta) | copy-start | bytes 393220
  153.2 17.3 %copy-start.40 = (f32[4,16,96]{2,1,0:T(8,128)}, f32[4,16,96]{2,1,0:T(8,128)S(1)}, u32[]{:S(2)}) copy-start(f32[4,16,96]{2,1,0:T(8,128)S(1)} %get-tuple-element.71.refs_4_) | copy-start | bytes 73732
  153.2 17.2 %copy-start.46 = (f32[16,16]{1,0:T(8,128)}, f32[16,16]{1,0:T(8,128)S(1)}, u32[]{:S(2)}) copy-start(f32[16,16]{1,0:T(8,128)S(1)} %get-tuple-element.70.refs_2_) | copy-start | bytes 3076
  170.7 0.7 copy-start.20
  171.4 13.2 %all-to-all-start.7 = ((bf16[72,16,128]{2,1,0:T(8,128)(2,1)}), bf16[72,16,128]{2,1,0:T(8,128)(2,1)S(1)}, u32[]{:S(2)}, u32[]{:S(2)}) async-start(bf16[72,16,128]{2,1,0:T(8,128)(2,1)} %copy-done.20), calls=%async_computation.7 | async-start | bytes 589824 | tf_op jit(solution)/shard_map/all_to_all | solution.py:349
  174.8 1.0 copy-start.3
  175.9 1.0 copy-start.10
  176.9 0.8 copy-start.23
  177.8 0.9 copy-start.29
  178.7 0.9 copy-start.31
  179.6 0.9 copy-start.39
  181.5 0.8 copy-start.12
  182.3 0.8 copy-start.17
  184.6 19.6 %copy-start.11 = (f32[64,16,128]{2,1,0:T(8,128)S(1)}, f32[64,16,128]{2,1,0:T(8,128)}, u32[]{:S(2)}) copy-start(f32[64,16,128]{2,1,0:T(8,128)} %copy-done.8) | copy-start | bytes 1572868
  204.2 1.0 copy-start.18
  208.9 0.8 copy-start.5
  209.7 18.2 %copy-start.26 = (f32[16,16,128]{2,1,0:T(8,128)}, f32[16,16,128]{2,1,0:T(8,128)S(1)}, u32[]{:S(2)}) copy-start(f32[16,16,128]{2,1,0:T(8,128)S(1)} %get-tuple-element.81.refs_3_) | copy-start | bytes 393220
  229.1 21.7 %copy-start.41 = (f32[4,16,96]{2,1,0:T(8,128)S(1)}, f32[4,16,96]{2,1,0:T(8,128)}, u32[]{:S(2)}) copy-start(f32[4,16,96]{2,1,0:T(8,128)} %copy-done.40) | copy-start | bytes 73732
  229.1 21.7 %copy-start.47 = (f32[16,16]{1,0:T(8,128)S(1)}, f32[16,16]{1,0:T(8,128)}, u32[]{:S(2)}) copy-start(f32[16,16]{1,0:T(8,128)} %copy-done.46) | copy-start | bytes 3076
  229.1 21.7 %all-to-all-start.9 = ((bf16[288,16,128]{2,1,0:T(8,128)(2,1)}), bf16[288,16,128]{2,1,0:T(8,128)(2,1)}, u32[]{:S(2)}, u32[]{:S(2)}) async-start(bf16[288,16,128]{2,1,0:T(8,128)(2,1)} %bitcast.27), calls=%async_computation.9 | async-start | bytes 2359296 | tf_op jit(solution)/shard_map/all_to_all | solution.py:368
  233.5 2.6 collective-permute-start.4
  234.8 5.4 %collective-permute-start.5 = (bf16[16,16,128]{2,1,0:T(8,128)(2,1)S(1)}, bf16[16,16,128]{2,1,0:T(8,128)(2,1)S(1)}, u32[]{:S(2)}, u32[]{:S(2)}) collective-permute-start(bf16[16,16,128]{2,1,0:T(8,128)(2,1)S(1)} %get-tuple-element.67), channel_id=1, source_target_pairs={{1,0},{2,1},{3,2},{4,3},{5,4},{6,5},{7,6},{8,7},{9,8},{10,9},{11,1... | collective-permute-start | bytes 196616 | tf_op jit(solution)/shard_map/ppermute | solution.py:366
  240.2 1.0 copy-start.6
  241.3 1.0 copy-start.19
  254.8 17.4 %copy-start.36 = (f32[16,16,128]{2,1,0:T(8,128)}, f32[16,16,128]{2,1,0:T(8,128)S(1)}, u32[]{:S(2)}) copy-start(f32[16,16,128]{2,1,0:T(8,128)S(1)} %get-tuple-element.76.beta) | copy-start | bytes 393220
  272.1 4.6 %copy-start.4 = (f32[4,16,16,128]{3,2,1,0:T(8,128)S(1)}, f32[4,16,16,128]{3,2,1,0:T(8,128)}, u32[]{:S(2)}) copy-start(f32[4,16,16,128]{3,2,1,0:T(8,128)} %copy-done) | copy-start | bytes 1572868
  272.1 4.6 %copy-start.13 = (f32[64,16,128]{2,1,0:T(8,128)S(1)}, f32[64,16,128]{2,1,0:T(8,128)}, u32[]{:S(2)}) copy-start(f32[64,16,128]{2,1,0:T(8,128)} %copy-done.12) | copy-start | bytes 1572868
  272.1 4.6 %copy-start.25 = (f32[16,16,128]{2,1,0:T(8,128)S(1)}, f32[16,16,128]{2,1,0:T(8,128)}, u32[]{:S(2)}) copy-start(f32[16,16,128]{2,1,0:T(8,128)} %copy-done.24) | copy-start | bytes 393220
  272.2 4.6 %copy-start.27 = (f32[16,16,128]{2,1,0:T(8,128)S(1)}, f32[16,16,128]{2,1,0:T(8,128)}, u32[]{:S(2)}) copy-start(f32[16,16,128]{2,1,0:T(8,128)} %copy-done.26) | copy-start | bytes 393220
  273.1 4.8 %copy-start.7 = (f32[64,16,128]{2,1,0:T(8,128)S(1)}, f32[64,16,128]{2,1,0:T(8,128)}, u32[]{:S(2)}) copy-start(f32[64,16,128]{2,1,0:T(8,128)} %copy-done.5) | copy-start | bytes 1572868
  273.1 4.8 %copy-start.33 = (f32[16,16,128]{2,1,0:T(8,128)S(1)}, f32[16,16,128]{2,1,0:T(8,128)}, u32[]{:S(2)}) copy-start(f32[16,16,128]{2,1,0:T(8,128)} %copy-done.32) | copy-start | bytes 393220
  273.1 13.4 %all-to-all-start.11 = ((bf16[72,16,128]{2,1,0:T(8,128)(2,1)}), bf16[72,16,128]{2,1,0:T(8,128)(2,1)S(1)}, u32[]{:S(2)}, u32[]{:S(2)}) async-start(bf16[72,16,128]{2,1,0:T(8,128)(2,1)} %shard_map.91), calls=%async_computation.11 | async-start | bytes 589824 | tf_op jit(solution)/shard_map/all_to_all | solution.py:349
  276.7 1.2 copy-start.35
  276.7 1.2 copy-start.37
  278.0 29.7 %copy-start.52 = (s32[128]{0:T(128)S(1)}, s32[128]{0:T(128)}, u32[]{:S(2)}) copy-start(s32[128]{0:T(128)} %copy-done.50) | copy-start | bytes 1540
  (7 other events, 4.5 us)
